TPU v7x, 32 devices: a whole 2x2x4 slice. The times are simulated.
32 devices in a mesh: row: 4 (over z), col: 8 (over y, x, core).
Axes of the slice: x: 2, y: 2, z: 4, core: 2. Of those that a mesh axis runs over, the one named last changes fastest.
Arguments:
- pair: bfloat16 [192, 192, 128], P('row', 'col'), may hold values from -6 to 6
- chain_tokens: int32 [8], replicated, may hold values from 6 to 24, as said below
- w_in: bfloat16 [128, 640], replicated, may hold values from -0.5 to 0.5
- w_out: bfloat16 [128, 128], replicated, may hold values from -0.5 to 0.5
- grad_update: bfloat16 [192, 192, 128], P('row', 'col'), may hold values from -6 to 6
Outputs:
- update: bfloat16 [192, 192, 128], P('row', 'col')
- grad_pair: bfloat16 [192, 192, 128], P('row', 'col')
Inputs may be any that keep to these rules, and one draw needn't show every extreme that they name: `chain_tokens`: one chain has exactly 24 real tokens and one has the fewest allowed.
All inputs are finite; a program needn't handle non-finite values.
Results may differ from a plain program's by a relative error of at most 0.014.
Values may be sent and summed in bfloat16 or wider, within the bound.
A program may use at most 256 MiB of HBM per device.

v0:
```python
import jax
import jax.numpy as jnp
from jax import lax
from jax.sharding import PartitionSpec as P


def normalize(values):
    mean = jnp.mean(values, axis=-1, keepdims=True)
    centred = values - mean
    rstd = 1.0 / jnp.sqrt(jnp.mean(centred * centred, axis=-1, keepdims=True) + 1e-05)
    return (centred * rstd, rstd)


def norm_back(grad, normed, rstd):
    return rstd * (
        grad
        - jnp.mean(grad, axis=-1, keepdims=True)
        - normed * jnp.mean(grad * normed, axis=-1, keepdims=True)
    )


def token_valid(positions, chain_tokens, slot):
    chain_of = positions // slot
    offset = positions - chain_of * slot
    onehot = chain_of[:, None] == jnp.arange(chain_tokens.shape[0], dtype=jnp.int32)[None, :]
    count = jnp.sum(jnp.where(onehot, chain_tokens[None, :], 0), axis=1)
    return (offset < count).astype(jnp.float32)


def reorder(panel, outer_count, inner_count):
    shape = panel.shape
    blocks = panel.reshape((outer_count, inner_count, -1) + shape[1:])
    return jnp.swapaxes(blocks, 0, 1).reshape(shape)


def on_device(pair, chain_tokens, w_in, w_out, grad_update):
    rows_count = lax.axis_size("row")
    cols_count = lax.axis_size("col")
    tile_i, tile_j, width = pair.shape
    tokens = tile_i * rows_count
    slot = tokens // chain_tokens.shape[0]
    row_pos = lax.axis_index("row") * tile_i + jnp.arange(tile_i, dtype=jnp.int32)
    col_pos = lax.axis_index("col") * tile_j + jnp.arange(tile_j, dtype=jnp.int32)
    mask = (
        token_valid(row_pos, chain_tokens, slot)[:, None]
        * token_valid(col_pos, chain_tokens, slot)[None, :]
    )[:, :, None]
    normed, rstd = normalize(pair.astype(jnp.float32))
    proj = jnp.einsum(
        "ijc,cd->ijd", normed.astype(jnp.bfloat16), w_in, preferred_element_type=jnp.float32
    )
    a_lin = proj[..., 0:width]
    a_gate = proj[..., width : 2 * width]
    b_lin = proj[..., 2 * width : 3 * width]
    b_gate = proj[..., 3 * width : 4 * width]
    o_gate = proj[..., 4 * width : 5 * width]
    s_a = jax.nn.sigmoid(a_gate)
    s_b = jax.nn.sigmoid(b_gate)
    s_o = jax.nn.sigmoid(o_gate)
    left = (mask * s_a * a_lin).astype(jnp.bfloat16)
    right = (mask * s_b * b_lin).astype(jnp.bfloat16)
    left_moved = lax.all_to_all(
        lax.all_to_all(left, "col", split_axis=0, concat_axis=1, tiled=True),
        "row",
        split_axis=1,
        concat_axis=0,
        tiled=True,
    )
    right_natural = lax.all_gather(right, "row", axis=0, tiled=True)
    right_sorted = reorder(right_natural, rows_count, cols_count)
    matched = right_sorted
    outer = jnp.einsum(
        "kic,kjc->ijc",
        lax.all_gather(left_moved, "col", axis=0, tiled=True),
        matched,
        preferred_element_type=jnp.float32,
    )
    onorm, orstd = normalize(outer)
    value = jnp.einsum(
        "ijc,cd->ijd", onorm.astype(jnp.bfloat16), w_out, preferred_element_type=jnp.float32
    )
    update = (s_o * value).astype(jnp.bfloat16)
    grad32 = grad_update.astype(jnp.float32)
    dvb = (grad32 * s_o).astype(jnp.bfloat16)
    du = jnp.einsum("ijd,cd->ijc", dvb, w_out, preferred_element_type=jnp.float32)
    dob = norm_back(du, onorm, orstd).astype(jnp.bfloat16)
    left_panel = lax.all_gather(left_moved, "col", axis=0, tiled=True)
    left_natural = reorder(left_panel, cols_count, rows_count)
    matched = right_sorted
    left_grad = lax.psum_scatter(
        jnp.einsum("ijc,kjc->kic", dob, matched, preferred_element_type=jnp.float32).astype(
            jnp.bfloat16
        ),
        "col",
        scatter_dimension=0,
        tiled=True,
    )
    left_home = lax.all_to_all(
        lax.all_to_all(left_grad, "row", split_axis=0, concat_axis=1, tiled=True),
        "col",
        split_axis=1,
        concat_axis=0,
        tiled=True,
    )
    matched = left_natural
    right_grad = lax.psum_scatter(
        jnp.einsum("ijc,kic->kjc", dob, matched, preferred_element_type=jnp.float32).astype(
            jnp.bfloat16
        ),
        "row",
        scatter_dimension=0,
        tiled=True,
    ).astype(jnp.float32)
    d_left = left_home.astype(jnp.float32) * mask
    d_right = right_grad * mask
    dproj = jnp.concatenate(
        [
            d_left * s_a,
            d_left * a_lin * s_a * (1.0 - s_a),
            d_right * s_b,
            d_right * b_lin * s_b * (1.0 - s_b),
            grad32 * value * s_o * (1.0 - s_o),
        ],
        axis=2,
    ).astype(jnp.bfloat16)
    dx = jnp.einsum("ijd,cd->ijc", dproj, w_in, preferred_element_type=jnp.float32)
    grad_pair = norm_back(dx, normed, rstd).astype(jnp.bfloat16)
    return (update, grad_pair)


def solution(mesh):
    return jax.shard_map(
        on_device,
        mesh=mesh,
        in_specs=(P("row", "col", None), P(), P(), P(), P("row", "col", None)),
        out_specs=(P("row", "col", None), P("row", "col", None)),
        check_vma=False,
    )
```

profile of v0, /device:TPU:0, one launch (start us, length us, event | category | flops | bytes accessed | tf_op | source)
XLA Modules:
  0.0 215.8 jit_solution(17515057766521173011)
XLA Ops:
  7.2 1.2 convert_reduce_fusion
  8.6 1.4 fusion.11
  11.7 1.8 fusion.30
  13.6 1.1 multiply_convert_fusion.6
  14.8 12.3 %all_to_all.63 = bf16[48,24,128]{2,1,0:T(8,128)(2,1)S(1)} all-to-all(bf16[48,24,128]{2,1,0:T(8,128)(2,1)S(1)} %get-tuple-element.6), channel_id=1, replica_groups=mesh['row'=4,'col'=8] {'col'}, dimensions={0} | all-to-all | bytes 589824 | tf_op jit(solution)/shard_map/all_to_all | solution.py:63
  27.3 27.4 %all_to_all.64 = bf16[6,192,128]{2,0,1:T(8,128)(2,1)S(1)} all-to-all(bf16[6,192,128]{2,0,1:T(8,128)(2,1)S(1)} %copy.144), channel_id=1, replica_groups=mesh['row'=4,'col'=8] {'row'}, dimensions={1} | all-to-all | bytes 589824 | tf_op jit(solution)/shard_map/all_to_all | solution.py:62
  54.7 1.2 copy.147
  56.0 2.2 %fusion.42 = (f32[48,24]{1,0:T(8,128)S(1)}, f32[48,24,128]{2,1,0:T(8,128)}) fusion(bf16[128,128]{1,0:T(8,128)(2,1)S(1)} %copy-done.10, bf16[48,24,128]{2,1,0:T(8,128)(2,1)} %param.9, f32[48,24,640]{2,1,0:T(8,128)S(1)} %fusion.30), kind=kOutput, calls=%fused_computation.84 | convolution fusion | flops 38779776 | bytes 1511936 | tf_op jit(solution)/shard_map/ijd,cd->ijc/dot_general | solution.py:85
  58.2 2.7 %copy.151 = f32[48,24,128]{0,1,2:T(8,128)} copy(f32[48,24,128]{2,1,0:T(8,128)} %get-tuple-element.14) | data formatting | bytes 1179648 | tf_op jit(solution)/shard_map/ijd,cd->ijc/dot_general | solution.py:85
  61.0 2.5 %copy.142 = bf16[8,4,6,24,128]{4,3,2,1,0:T(8,128)(2,1)} copy(bf16[8,4,6,24,128]{4,3,2,0,1:T(8,128)(2,1)} %bitcast.77) | data formatting | bytes 2359296 | tf_op jit(solution)/shard_map/transpose | solution.py:33
  63.5 3.4 %copy.148 = bf16[192,24,128]{0,1,2:T(8,128)(2,1)} copy(bf16[192,24,128]{2,1,0:T(8,128)(2,1)} %bitcast.75) | data formatting | bytes 2359296 | tf_op jit(solution)/shard_map/reshape | solution.py:33
  66.9 37.1 %all-gather.5.cloned.1.call-done = bf16[192,48,128]{1,0,2:T(8,128)(2,1)} async-done(((bf16[24,48,128]{1,0,2:T(8,128)(2,1)}), bf16[192,48,128]{1,0,2:T(8,128)(2,1)}) %all-gather.5.cloned.1.call-update) | async-done | bytes 2359312 | tf_op jit(solution)/shard_map/all_gather | solution.py:74
  104.0 5.0 %bitcast_reduce_fusion = (f32[48,24]{0,1:T(8,128)S(1)}, f32[128,24,48]{2,1,0:T(8,128)S(1)}) fusion(bf16[192,24,128]{0,1,2:T(8,128)(2,1)} %copy.148, bf16[192,48,128]{1,0,2:T(8,128)(2,1)} %all-gather.5.cloned.1.call-done), kind=kOutput, calls=%fused_computation.2 | convolution fusion | flops 56769408 | bytes 4133376 | tf_op jit(solution)/shard_map/kic,kjc->ijc/dot_general | solution.py:72
  109.4 1.1 copy-done.2
  110.8 1.3 multiply_convert_fusion
  113.1 2.7 %convert_bitcast_fusion = bf16[192,48,128]{0,1,2:T(8,128)(2,1)} fusion(bf16[192,24,128]{0,1,2:T(8,128)(2,1)S(1)} %copy-done.1, bf16[48,24,128]{0,1,2:T(8,128)(2,1)S(1)} %get-tuple-element.9), kind=kOutput, calls=%fused_computation | convolution fusion | flops 57802752 | bytes 3833856 | tf_op jit(solution)/shard_map/ijc,kjc->kic/dot_general | solution.py:91
  115.8 5.4 %copy.154 = bf16[192,48,128]{2,1,0:T(8,128)(2,1)} copy(bf16[192,48,128]{0,1,2:T(8,128)(2,1)} %convert_bitcast_fusion) | data formatting | bytes 4718592 | tf_op jit(solution)/shard_map/convert_element_type | solution.py:91
  121.4 9.0 %copy.159 = bf16[192,48,128]{2,1,0:T(8,128)(2,1)} copy(bf16[192,48,128]{1,0,2:T(8,128)(2,1)} %all-gather.5.cloned.1.call-done) | data formatting | bytes 4718592 | tf_op jit(solution)/shard_map/all_gather | solution.py:74
  130.4 3.7 %copy.160 = bf16[4,8,6,48,128]{4,3,2,1,0:T(8,128)(2,1)} copy(bf16[4,8,6,48,128]{4,3,2,0,1:T(8,128)(2,1)} %bitcast.72) | data formatting | bytes 4718592 | tf_op jit(solution)/shard_map/transpose | solution.py:33
  134.1 5.4 %copy.161 = bf16[192,48,128]{0,1,2:T(8,128)(2,1)} copy(bf16[192,48,128]{2,1,0:T(8,128)(2,1)} %bitcast.73) | data formatting | bytes 4718592 | tf_op jit(solution)/shard_map/reshape | solution.py:33
  139.5 3.8 %fusion.43 = bf16[128,192,24]{1,2,0:T(8,128)(2,1)} fusion(bf16[192,48,128]{0,1,2:T(8,128)(2,1)} %copy.161, bf16[48,24,128]{0,1,2:T(8,128)(2,1)} %copy-done.3), kind=kOutput, calls=%fused_computation.85 | convolution fusion | flops 56623104 | bytes 3833856 | tf_op jit(solution)/shard_map/ijc,kic->kjc/dot_general | solution.py:107
  143.3 3.1 %copy.162 = bf16[128,192,24]{0,2,1:T(8,128)(2,1)} copy(bf16[128,192,24]{1,2,0:T(8,128)(2,1)} %fusion.43) | data formatting | bytes 2359296 | tf_op jit(solution)/shard_map/ijc,kic->kjc/dot_general | solution.py:107
  146.4 17.4 %reduce-scatter.3.cloned.1.call-done = bf16[24,48,128]{2,1,0:T(8,128)(2,1)} async-done(((bf16[192,48,128]{2,1,0:T(8,128)(2,1)}), bf16[24,48,128]{2,1,0:T(8,128)(2,1)}) %reduce-scatter.3.cloned.1.call-update) | async-done | bytes 294928 | tf_op jit(solution)/shard_map/reduce_scatter | solution.py:90
  163.9 19.9 %all_to_all.65 = bf16[24,48,128]{2,1,0:T(8,128)(2,1)S(1)} all-to-all(bf16[24,48,128]{2,1,0:T(8,128)(2,1)} %reduce-scatter.3.cloned.1.call-done), channel_id=1, replica_groups=mesh['row'=4,'col'=8] {'row'}, dimensions={0} | all-to-all | bytes 589824 | tf_op jit(solution)/shard_map/all_to_all | solution.py:99
  184.7 3.5 %all-to-all-start.3 = ((bf16[6,192,128]{2,0,1:T(8,128)(2,1)}), bf16[6,192,128]{2,0,1:T(8,128)(2,1)S(1)}, u32[]{:S(2)}, u32[]{:S(2)}) async-start(bf16[6,192,128]{2,0,1:T(8,128)(2,1)} %copy.156), calls=%async_computation.4 | async-start | bytes 786432 | tf_op jit(solution)/shard_map/all_to_all | solution.py:98
  188.2 2.4 %copy.149 = bf16[48,24,128]{2,1,0:T(8,128)(2,1)} copy(bf16[48,24,128]{0,1,2:T(8,128)(2,1)} %get-tuple-element.10) | data formatting | bytes 589824 | tf_op jit(solution)/shard_map/convert_element_type | solution.py:80
  190.5 5.9 %all-to-all-done.3 = bf16[6,192,128]{2,0,1:T(8,128)(2,1)S(1)} async-done(((bf16[6,192,128]{2,0,1:T(8,128)(2,1)}), bf16[6,192,128]{2,0,1:T(8,128)(2,1)S(1)}, u32[]{:S(2)}, u32[]{:S(2)}) %all-to-all-start.3) | async-done | bytes 294944 | tf_op jit(solution)/shard_map/all_to_all | solution.py:98
  197.4 1.3 multiply_convert_fusion.3
  200.4 2.0 fusion.25
  202.4 2.1 fusion.26
  205.4 2.1 fusion.41
  207.8 1.4 fusion.10
  (70 shorter events, 9.1 us)
Async XLA Ops:
  7.2 4.6 %copy-start = (bf16[128,640]{1,0:T(8,128)(2,1)S(1)}, bf16[128,640]{1,0:T(8,128)(2,1)}, u32[]{:S(2)}) copy-start(bf16[128,640]{1,0:T(8,128)(2,1)} %param.7) | copy-start | bytes 491524
  7.2 53.8 %all-gather.3.cloned.1.call-start = ((), (), s32[]{:S(2)}) async-start(), calls=%async_computation.6 | async-start | bytes 1474560 | tf_op jit(solution)/shard_map/all_gather | solution.py:69
  10.1 3.4 %copy-start.8 = (f32[48,24]{1,0:T(8,128)}, f32[48,24]{1,0:T(8,128)S(1)}, u32[]{:S(2)}) copy-start(f32[48,24]{1,0:T(8,128)S(1)} %copy.141) | copy-start | bytes 13828
  14.7 89.3 %all-gather.5.cloned.1.call-start = ((), (), s32[]{:S(2)}) async-start(), calls=%async_computation.7 | async-start | bytes 7077888 | tf_op jit(solution)/shard_map/all_gather | solution.py:74
  27.3 28.8 %copy-start.10 = (bf16[128,128]{1,0:T(8,128)(2,1)S(1)}, bf16[128,128]{1,0:T(8,128)(2,1)}, u32[]{:S(2)}) copy-start(bf16[128,128]{1,0:T(8,128)(2,1)} %param.8) | copy-start | bytes 98308
  56.0 107.9 %reduce-scatter.3.cloned.1.call-start = ((), (), s32[]{:S(2)}) async-start(), calls=%async_computation.8 | async-start | bytes 2654208 | tf_op jit(solution)/shard_map/reduce_scatter | solution.py:90
  109.1 1.4 copy-start.2
  110.8 2.3 %copy-start.1 = (bf16[192,24,128]{0,1,2:T(8,128)(2,1)S(1)}, bf16[192,24,128]{0,1,2:T(8,128)(2,1)}, u32[]{:S(2)}) copy-start(bf16[192,24,128]{0,1,2:T(8,128)(2,1)} %copy.148) | copy-start | bytes 3538948
  112.2 0.9 copy-start.3
  121.2 79.1 %reduce-scatter.5.cloned.1.call-start = ((), (), s32[]{:S(2)}) async-start(), calls=%async_computation.9 | async-start | bytes 1474560 | tf_op jit(solution)/shard_map/reduce_scatter | solution.py:106
  184.7 11.7 %all-to-all-start.3 = ((bf16[6,192,128]{2,0,1:T(8,128)(2,1)}), bf16[6,192,128]{2,0,1:T(8,128)(2,1)S(1)}, u32[]{:S(2)}, u32[]{:S(2)}) async-start(bf16[6,192,128]{2,0,1:T(8,128)(2,1)} %copy.156), calls=%async_computation.4 | async-start | bytes 786432 | tf_op jit(solution)/shard_map/all_to_all | solution.py:98
  196.4 1.0 copy-start.7
  196.4 1.0 copy-start.11
  200.4 4.1 %copy-start.5 = (f32[48,24,128]{2,1,0:T(8,128)S(1)}, f32[48,24,128]{2,1,0:T(8,128)}, u32[]{:S(2)}) copy-start(f32[48,24,128]{2,1,0:T(8,128)} %get-tuple-element.15) | copy-start | bytes 1769476
  200.4 4.1 %copy-start.6 = (bf16[48,24,128]{2,1,0:T(8,128)(2,1)S(1)}, bf16[48,24,128]{2,1,0:T(8,128)(2,1)}, u32[]{:S(2)}) copy-start(bf16[48,24,128]{2,1,0:T(8,128)(2,1)} %param.9) | copy-start | bytes 884740
  202.4 3.0 %copy-start.4 = (bf16[48,24,128]{2,1,0:T(8,128)(2,1)S(1)}, bf16[48,24,128]{2,1,0:T(8,128)(2,1)}, u32[]{:S(2)}) copy-start(bf16[48,24,128]{2,1,0:T(8,128)(2,1)} %param.5) | copy-start | bytes 884740
  202.4 3.0 %copy-start.9 = (f32[48,24]{1,0:T(8,128)S(1)}, f32[48,24]{1,0:T(8,128)}, u32[]{:S(2)}) copy-start(f32[48,24]{1,0:T(8,128)} %copy-done.8) | copy-start | bytes 13828
Sparse Core Ops, SparseCore 0:
  14.8 41.7 all-gather.2
  58.5 45.5 all-gather.4
  121.3 42.4 reduce-scatter.2
  166.1 30.4 reduce-scatter.4
where the time goes:
time: 217 us; the launch traced here: 216 us
  waiting for transfers between devices  60.5 us (28%)
  blocking collectives  59.5 us (27%)
  local copies, waits for them, and re-layouts  45.2 us (21%)
  matrix products  19 us (9%)
  between operations  13.9 us (6%)
  other arithmetic  13.8 us (6%)
  starting transfers between devices  3.8 us (2%)
    all_gather x1, waiting for transfers between devices, on_device(): lax.all_gather(left_moved, 'col', axis=0, tiled=True)  37.1 us
    all_to_all x1, blocking collectives, on_device(): lax.all_to_all(lax.all_to_all(left, 'col', split_axis=0, concat_axis=1, t...  27.4 us
    all_to_all x1, blocking collectives, on_device(): lax.all_to_all(left_grad, 'row', split_axis=0, concat_axis=1, tiled=True)  19.9 us
    reduce_scatter x1, waiting for transfers between devices, on_device(): lax.psum_scatter(jnp.einsum('ijc,kjc->kic', dob, matched, preferred_eleme...  17.4 us
    all_to_all x1, blocking collectives, on_device(): lax.all_to_all(left, 'col', split_axis=0, concat_axis=1, tiled=True)  12.3 us
    all_gather x1, local copies, waits for them, and re-layouts, on_device(): lax.all_gather(left_moved, 'col', axis=0, tiled=True)  8.95 us
    reshape x2, local copies, waits for them, and re-layouts, reorder(): return jnp.swapaxes(blocks, 0, 1).reshape(shape)  8.82 us
    transpose x2, local copies, waits for them, and re-layouts, reorder(): return jnp.swapaxes(blocks, 0, 1).reshape(shape)  6.18 us
  transfers between devices with their start and end apart: 5, of which 3 were waited for; matrix products, arithmetic and copies ran while one was open for 20% of the time, Pallas kernels for 0%

commit v1 on v0

v1 whole, which is shorter than its diff:
```python
import functools

import jax
import jax.numpy as jnp
from jax import lax
from jax.experimental import pallas as pl
from jax.experimental.pallas import tpu as pltpu
from jax.sharding import PartitionSpec as P

USE_XLA = False


def normalize(values):
    mean = jnp.mean(values, axis=-1, keepdims=True)
    centred = values - mean
    rstd = 1.0 / jnp.sqrt(jnp.mean(centred * centred, axis=-1, keepdims=True) + 1e-05)
    return (centred * rstd, rstd)


def norm_back(grad, normed, rstd):
    return rstd * (
        grad
        - jnp.mean(grad, axis=-1, keepdims=True)
        - normed * jnp.mean(grad * normed, axis=-1, keepdims=True)
    )


def token_valid(positions, chain_tokens, slot):
    chain_of = positions // slot
    offset = positions - chain_of * slot
    onehot = chain_of[:, None] == jnp.arange(chain_tokens.shape[0], dtype=jnp.int32)[None, :]
    count = jnp.sum(jnp.where(onehot, chain_tokens[None, :], 0), axis=1)
    return (offset < count).astype(jnp.float32)


def exchange_kernel(rows, cols, src, dst, send_sem, recv_sem, own_sem):
    total = rows * cols
    me = lax.axis_index("row") * cols + lax.axis_index("col")
    barrier = pltpu.get_barrier_semaphore()

    def greet(step, carry):
        peer = lax.rem(me + step, total)
        pl.semaphore_signal(
            barrier,
            inc=1,
            device_id=(peer // cols, lax.rem(peer, cols)),
            device_id_type=pl.DeviceIdType.MESH,
        )
        return carry

    own = pltpu.make_async_copy(src.at[me], dst.at[me], own_sem)
    own.start()
    lax.fori_loop(1, total, greet, 0)
    pl.semaphore_wait(barrier, total - 1)

    def copy_to(step):
        peer = lax.rem(me + step, total)
        return pltpu.make_async_remote_copy(
            src_ref=src.at[peer],
            dst_ref=dst.at[me],
            send_sem=send_sem.at[peer],
            recv_sem=recv_sem.at[me],
            device_id=(peer // cols, lax.rem(peer, cols)),
            device_id_type=pl.DeviceIdType.MESH,
        )

    def copy_from(step):
        peer = lax.rem(me + step, total)
        return pltpu.make_async_remote_copy(
            src_ref=src.at[peer],
            dst_ref=dst.at[peer],
            send_sem=send_sem.at[peer],
            recv_sem=recv_sem.at[peer],
            device_id=(peer // cols, lax.rem(peer, cols)),
            device_id_type=pl.DeviceIdType.MESH,
        )

    def send(step, carry):
        copy_to(step).start()
        return carry

    def finish(step, carry):
        copy = copy_from(step)
        copy.wait_send()
        copy.wait_recv()
        return carry

    lax.fori_loop(1, total, send, 0)
    own.wait()
    lax.fori_loop(1, total, finish, 0)


def exchange(blocks, rows, cols, call):
    total = rows * cols
    shape = blocks.shape
    if USE_XLA:
        return lax.all_to_all(blocks, ("row", "col"), split_axis=0, concat_axis=0, tiled=True)
    flat = blocks.reshape(total, -1, 128)
    moved = pl.pallas_call(
        functools.partial(exchange_kernel, rows, cols),
        out_shape=jax.ShapeDtypeStruct(flat.shape, flat.dtype),
        in_specs=[pl.BlockSpec(memory_space=pl.ANY)],
        out_specs=pl.BlockSpec(memory_space=pl.ANY),
        scratch_shapes=[
            pltpu.SemaphoreType.DMA((total,)),
            pltpu.SemaphoreType.DMA((total,)),
            pltpu.SemaphoreType.DMA,
        ],
        compiler_params=pltpu.CompilerParams(collective_id=call, has_side_effects=True),
        name="exchange",
    )(flat)
    return moved.reshape(shape)


def on_device(pair, chain_tokens, w_in, w_out, grad_update):
    rows = lax.axis_size("row")
    cols = lax.axis_size("col")
    tile_i, tile_j, width = pair.shape
    tokens = tile_i * rows
    devices = rows * cols
    own = width // devices
    slot = tokens // chain_tokens.shape[0]

    def to_planes(arrays, call):
        count = len(arrays)
        blocks = jnp.stack([a.reshape(tile_i, tile_j, devices, own) for a in arrays])
        blocks = blocks.transpose(3, 0, 4, 1, 2)
        moved = exchange(blocks, rows, cols, call)
        moved = moved.reshape(rows, cols, count, own, tile_i, tile_j).transpose(2, 3, 0, 4, 1, 5)
        return moved.reshape(count, own, tokens, tokens)

    def to_tiles(planes, call):
        count = len(planes)
        blocks = jnp.stack([p.reshape(own, rows, tile_i, cols, tile_j) for p in planes])
        blocks = blocks.transpose(2, 4, 0, 1, 3, 5).reshape(devices, count, own, tile_i, tile_j)
        moved = exchange(blocks, rows, cols, call)
        return moved.transpose(1, 3, 4, 0, 2).reshape(count, tile_i, tile_j, width)

    row_pos = lax.axis_index("row") * tile_i + jnp.arange(tile_i, dtype=jnp.int32)
    col_pos = lax.axis_index("col") * tile_j + jnp.arange(tile_j, dtype=jnp.int32)
    mask = (
        token_valid(row_pos, chain_tokens, slot)[:, None]
        * token_valid(col_pos, chain_tokens, slot)[None, :]
    )[:, :, None]
    normed, rstd = normalize(pair.astype(jnp.float32))
    proj = jnp.einsum(
        "ijc,cd->ijd", normed.astype(jnp.bfloat16), w_in, preferred_element_type=jnp.float32
    )
    a_lin, a_gate, b_lin, b_gate, o_gate = (
        proj[..., n * width : (n + 1) * width] for n in range(5)
    )
    s_a = jax.nn.sigmoid(a_gate)
    s_b = jax.nn.sigmoid(b_gate)
    s_o = jax.nn.sigmoid(o_gate)
    left = (mask * s_a * a_lin).astype(jnp.bfloat16)
    right = (mask * s_b * b_lin).astype(jnp.bfloat16)
    planes = to_planes([left, right], 0)
    left_p, right_p = planes[0], planes[1]
    outer_p = jnp.einsum("cki,ckj->cij", left_p, right_p, preferred_element_type=jnp.float32)
    outer = to_tiles([outer_p.astype(jnp.bfloat16)], 1)[0].astype(jnp.float32)
    onorm, orstd = normalize(outer)
    value = jnp.einsum(
        "ijc,cd->ijd", onorm.astype(jnp.bfloat16), w_out, preferred_element_type=jnp.float32
    )
    update = (s_o * value).astype(jnp.bfloat16)
    grad32 = grad_update.astype(jnp.float32)
    dvb = (grad32 * s_o).astype(jnp.bfloat16)
    du = jnp.einsum("ijd,cd->ijc", dvb, w_out, preferred_element_type=jnp.float32)
    dob = norm_back(du, onorm, orstd).astype(jnp.bfloat16)
    dob_p = to_planes([dob], 2)[0]
    dleft_p = jnp.einsum("cij,ckj->cki", dob_p, right_p, preferred_element_type=jnp.float32)
    dright_p = jnp.einsum("cij,cki->ckj", dob_p, left_p, preferred_element_type=jnp.float32)
    grads = to_tiles([dleft_p.astype(jnp.bfloat16), dright_p.astype(jnp.bfloat16)], 3)
    d_left = grads[0].astype(jnp.float32) * mask
    d_right = grads[1].astype(jnp.float32) * mask
    dproj = jnp.concatenate(
        [
            d_left * s_a,
            d_left * a_lin * s_a * (1.0 - s_a),
            d_right * s_b,
            d_right * b_lin * s_b * (1.0 - s_b),
            grad32 * value * s_o * (1.0 - s_o),
        ],
        axis=2,
    ).astype(jnp.bfloat16)
    dx = jnp.einsum("ijd,cd->ijc", dproj, w_in, preferred_element_type=jnp.float32)
    grad_pair = norm_back(dx, normed, rstd).astype(jnp.bfloat16)
    return (update, grad_pair)


def solution(mesh):
    return jax.shard_map(
        on_device,
        mesh=mesh,
        in_specs=(P("row", "col", None), P(), P(), P(), P("row", "col", None)),
        out_specs=(P("row", "col", None), P("row", "col", None)),
        check_vma=False,
    )
```

time: 217 us -> 186 us (0.86)
  the two profiles are of different devices: /device:TPU:0 before, /device:TPU:15 now
where the time goes in v1:
time: 186 us; the launch traced here: 185 us
  local copies, waits for them, and re-layouts  87.6 us (47%)
  Pallas kernels  66.7 us (36%)
  other arithmetic  18.5 us (10%)
  matrix products  10.8 us (6%)
    pallas_call x4, Pallas kernels, exchange(): pl.pallas_call(functools.partial(exchange_kernel, rows, cols), out_shape=...  66.7 us
    reshape x2, local copies, waits for them, and re-layouts, exchange(): return moved.reshape(shape)  11.6 us
    another operation x2, local copies, waits for them, and re-layouts, to_planes(): moved.reshape(rows, cols, count, own, tile_i, tile_j)  9.45 us
    another operation x2, local copies, waits for them, and re-layouts, exchange(): flat = blocks.reshape(total, -1, 128)  9.14 us
    reshape x2, local copies, waits for them, and re-layouts, exchange(): flat = blocks.reshape(total, -1, 128)  8.99 us
    convert_element_type x2, local copies, waits for them, and re-layouts, on_device(): d_left = grads[0].astype(jnp.float32) * mask  6.13 us
    transpose x2, local copies, waits for them, and re-layouts, to_tiles(): blocks.transpose(2, 4, 0, 1, 3, 5)  5.3 us
    slice x3, local copies, waits for them, and re-layouts, on_device(): left_p, right_p = (planes[0], planes[1])  5.28 us

profile of v1, /device:TPU:15, one launch (start us, length us, event | category | flops | bytes accessed | tf_op | source)
XLA Modules:
  0.0 184.6 jit_solution(15033495830411601955)
XLA Ops:
  5.5 1.8 fusion.35
  11.8 3.1 %copy.70 = bf16[32,2,4,48,24]{4,3,2,1,0:T(8,128)(2,1)S(1)} copy(bf16[32,2,4,48,24]{3,4,2,0,1:T(8,128)(2,1)} %maximum_bitcast_fusion) | data formatting | bytes 1179648 | tf_op jit(solution)/shard_map/transpose | solution.py:127
  14.9 4.9 %reshape.154.src = bf16[32,72,128]{2,1,0:T(8,128)(2,1)} reshape(bf16[32,2,4,48,24]{4,3,2,1,0:T(8,128)(2,1)S(1)} %copy.70) | data formatting | bytes 1179648 | tf_op jit(solution)/shard_map/reshape | solution.py:98
  19.8 20.0 %exchange.4 = bf16[32,72,128]{2,1,0:T(8,128)(2,1)} custom-call(bf16[32,72,128]{2,1,0:T(8,128)(2,1)} %reshape.154.src), custom_call_target="tpu_custom_call" | custom-call | tf_op jit(solution)/shard_map/exchange/pallas_call | solution.py:99
  39.8 5.4 %reshape_reshape.12 = bf16[4,8,2,4,48,24]{5,4,3,2,1,0:T(8,128)(2,1)S(1)} reshape(bf16[32,72,128]{2,1,0:T(8,128)(2,1)} %exchange.4) | data formatting | bytes 1179648 | tf_op jit(solution)/shard_map/reshape;reshape | solution.py:129
  45.2 2.4 %fusion.49 = (bf16[1,4,4,48,8,24]{5,3,1,0,4,2:T(8,128)(2,1)}, bf16[1,4,4,48,8,24]{5,3,1,0,4,2:T(8,128)(2,1)}) fusion(bf16[2,4,4,48,8,24]{5,3,1,0,4,2:T(8,128)(2,1)S(1)} %bitcast.72), kind=kLoop, calls=%fused_computation.90 | loop fusion | bytes 1179648 | tf_op jit(solution)/shard_map/slice | solution.py:158
  47.6 2.0 %copy.72 = bf16[1,4,4,48,8,24]{3,2,5,4,1,0:T(4,128)(2,1)S(1)} copy(bf16[1,4,4,48,8,24]{5,3,1,0,4,2:T(8,128)(2,1)} %get-tuple-element.6) | data formatting | bytes 589824 | tf_op jit(solution)/shard_map/slice | solution.py:158
  53.2 3.0 %reshape_reshape.13.src = bf16[32,36,128]{2,1,0:T(8,128)(2,1)} reshape(bf16[4,8,1,4,48,24]{5,4,3,1,0,2:T(8,128)(2,1)S(1)} %copy.75) | data formatting | bytes 589824 | tf_op jit(solution)/shard_map/reshape;reshape | solution.py:98
  56.2 13.7 %exchange.5 = bf16[32,36,128]{2,1,0:T(8,128)(2,1)} custom-call(bf16[32,36,128]{2,1,0:T(8,128)(2,1)} %reshape_reshape.13.src), custom_call_target="tpu_custom_call" | custom-call | tf_op jit(solution)/shard_map/exchange/pallas_call | solution.py:99
  69.9 3.0 %reshape.161 = f32[32,1,4,48,24]{4,3,2,0,1:T(8,128)S(1)} reshape(bf16[32,36,128]{2,1,0:T(8,128)(2,1)} %exchange.5) | data formatting | bytes 884736 | tf_op jit(solution)/shard_map/convert_element_type | solution.py:160
  73.6 1.8 copy.77
  75.5 2.2 %fusion.48 = (f32[48,24]{1,0:T(8,128)S(1)}, f32[48,24]{1,0:T(8,128)S(1)}, f32[48,24,128]{2,1,0:T(8,128)S(1)}) fusion(f32[48,24]{1,0:T(8,128)S(1)} %add_rsqrt_fusion, f32[48,24,128]{2,1,0:T(8,128)} %copy.77, f32[48,24]{1,0:T(8,128)S(1)} %broadcast_multiply_fusion.5, bf16[128,128]{1,0:T(8,128)(2,1)S(1)} %copy-done.15, bf16[48,24,128]{2,1,0:T(8,128)(2,1)} %param.9, ...), kind=kOutput, calls=%fused_computation.89 | convolution fusion | flops 39368448 | bytes 2115584 | tf_op jit(solution)/shard_map/ijd,cd->ijc/dot_general | solution.py:168
  82.0 4.1 %reshape.155.src = bf16[32,36,128]{2,1,0:T(8,128)(2,1)} reshape(bf16[32,1,4,48,24]{4,3,2,0,1:T(8,128)(2,1)} %bitcast.75) | data formatting | bytes 589824 | tf_op jit(solution)/shard_map/reshape | solution.py:98
  86.1 13.8 %exchange.6 = bf16[32,36,128]{2,1,0:T(8,128)(2,1)} custom-call(bf16[32,36,128]{2,1,0:T(8,128)(2,1)} %reshape.155.src), custom_call_target="tpu_custom_call" | custom-call | tf_op jit(solution)/shard_map/exchange/pallas_call | solution.py:99
  99.9 4.0 %reshape_reshape.14 = bf16[4,8,1,4,48,24]{5,4,3,1,0,2:T(8,128)(2,1)} reshape(bf16[32,36,128]{2,1,0:T(8,128)(2,1)} %exchange.6) | data formatting | bytes 589824 | tf_op jit(solution)/shard_map/reshape;reshape | solution.py:129
  103.9 2.6 %copy.80 = bf16[1,4,4,48,8,24]{3,2,5,4,1,0:T(4,128)(2,1)} copy(bf16[1,4,4,48,8,24]{5,3,1,4,2,0:T(8,128)(2,1)} %bitcast.76) | data formatting | bytes 589824 | tf_op jit(solution)/shard_map/transpose | solution.py:129
  106.5 2.4 %squeeze_reshape.4 = bf16[4,192,192]{1,2,0:T(8,128)(2,1)} reshape(bf16[1,4,4,48,8,24]{3,2,5,4,1,0:T(4,128)(2,1)} %copy.80) | data formatting | bytes 589824 | tf_op jit(solution)/shard_map/squeeze;reshape | solution.py:170
  108.9 2.2 %convolution_convert_fusion = bf16[4,192,192]{2,1,0:T(8,128)(2,1)} fusion(bf16[4,192,192]{1,2,0:T(8,128)(2,1)} %copy-done.9, bf16[4,192,192]{1,2,0:T(8,128)(2,1)} %squeeze_reshape.4), kind=kOutput, calls=%fused_computation.6 | convolution fusion | flops 56770560 | bytes 884736 | tf_op jit(solution)/shard_map/cij,cki->ckj/dot_general | solution.py:172
  111.1 2.1 %convolution_convert_fusion.1 = bf16[4,192,192]{2,1,0:T(8,128)(2,1)} fusion(bf16[4,192,192]{1,2,0:T(8,128)(2,1)S(1)} %copy-done.8, bf16[4,192,192]{1,2,0:T(8,128)(2,1)} %squeeze_reshape.4), kind=kOutput, calls=%fused_computation.7 | convolution fusion | flops 56770560 | bytes 884736 | tf_op jit(solution)/shard_map/cij,ckj->cki/dot_general | solution.py:171
  114.5 1.9 %copy.86 = bf16[4,192,192]{1,2,0:T(8,128)(2,1)} copy(bf16[4,192,192]{2,1,0:T(8,128)(2,1)} %convolution_convert_fusion) | data formatting | bytes 589824 | tf_op jit(solution)/shard_map/convert_element_type | solution.py:173
  116.4 2.7 %stack_reshape.23 = bf16[1,4,4,48,8,24]{3,2,5,4,1,0:T(4,128)(2,1)} reshape(bf16[4,192,192]{1,2,0:T(8,128)(2,1)} %copy.86) | data formatting | bytes 589824 | tf_op jit(solution)/shard_map/stack;reshape | solution.py:134
  120.4 3.8 %maximum_bitcast_fusion.1 = bf16[4,8,2,4,48,24]{4,0,5,1,3,2:T(4,128)(2,1)} fusion(bf16[1,4,4,48,8,24]{3,2,5,4,1,0:T(4,128)(2,1)} %stack_reshape.23, bf16[1,4,4,48,8,24]{3,2,5,4,1,0:T(4,128)(2,1)} %stack_reshape.22), kind=kLoop, calls=%fused_computation.5 | loop fusion | flops 294912 | bytes 1179648 | tf_op jit(solution)/shard_map/transpose | solution.py:135
  124.2 4.4 %copy.87 = bf16[4,8,2,4,48,24]{5,4,3,2,1,0:T(8,128)(2,1)} copy(bf16[4,8,2,4,48,24]{4,0,5,1,3,2:T(4,128)(2,1)} %maximum_bitcast_fusion.1) | data formatting | bytes 1179648 | tf_op jit(solution)/shard_map/transpose | solution.py:135
  128.6 6.2 %reshape_reshape.15.src = bf16[32,72,128]{2,1,0:T(8,128)(2,1)} reshape(bf16[4,8,2,4,48,24]{5,4,3,2,1,0:T(8,128)(2,1)} %copy.87) | data formatting | bytes 1179648 | tf_op jit(solution)/shard_map/reshape;reshape | solution.py:98
  134.8 19.2 %exchange.7 = bf16[32,72,128]{2,1,0:T(8,128)(2,1)} custom-call(bf16[32,72,128]{2,1,0:T(8,128)(2,1)} %reshape_reshape.15.src), custom_call_target="tpu_custom_call" | custom-call | tf_op jit(solution)/shard_map/exchange/pallas_call | solution.py:99
  154.0 6.5 %reshape.156 = bf16[32,2,4,48,24]{4,3,2,1,0:T(8,128)(2,1)} reshape(bf16[32,72,128]{2,1,0:T(8,128)(2,1)} %exchange.7) | data formatting | bytes 1179648 | tf_op jit(solution)/shard_map/reshape | solution.py:112
  160.5 5.1 %copy.88 = bf16[32,2,4,48,24]{3,0,2,4,1:T(8,128)(2,1)} copy(bf16[32,2,4,48,24]{4,3,2,1,0:T(8,128)(2,1)} %reshape.156) | data formatting | bytes 1179648 | tf_op jit(solution)/shard_map/reshape | solution.py:112
  165.6 2.8 %slice_convert_fusion = (f32[1,48,24,32,4]{1,3,4,2,0:T(8,128)S(1)}, f32[1,48,24,32,4]{1,3,4,2,0:T(8,128)}) fusion(bf16[2,48,24,32,4]{1,3,4,2,0:T(8,128)(2,1)} %bitcast.77), kind=kLoop, calls=%fused_computation.9 | loop fusion | flops 294912 | bytes 1769472 | tf_op jit(solution)/shard_map/convert_element_type | solution.py:175
  168.4 2.1 %copy.91 = f32[1,48,24,32,4]{1,2,4,3,0:T(8,128)} copy(f32[1,48,24,32,4]{1,3,4,2,0:T(8,128)S(1)} %get-tuple-element.10) | data formatting | bytes 1179648 | tf_op jit(solution)/shard_map/convert_element_type | solution.py:175
  170.5 2.7 %copy.92 = f32[48,24,128]{2,1,0:T(8,128)} copy(f32[48,24,128]{0,1,2:T(8,128)} %bitcast.73) | data formatting | bytes 1179648 | tf_op jit(solution)/shard_map/convert_element_type | solution.py:175
  173.2 3.5 %copy.89 = f32[1,48,24,32,4]{1,2,4,3,0:T(8,128)} copy(f32[1,48,24,32,4]{1,3,4,2,0:T(8,128)} %get-tuple-element.11) | data formatting | bytes 1179648 | tf_op jit(solution)/shard_map/convert_element_type | solution.py:174
  176.6 2.7 %copy.90 = f32[48,24,128]{2,1,0:T(8,128)} copy(f32[48,24,128]{0,1,2:T(8,128)} %bitcast.74) | data formatting | bytes 1179648 | tf_op jit(solution)/shard_map/convert_element_type | solution.py:174
  (75 shorter events, 25.4 us)
Async XLA Ops:
  0.6 4.9 %copy-start = (bf16[128,640]{1,0:T(8,128)(2,1)S(1)}, bf16[128,640]{1,0:T(8,128)(2,1)}, u32[]{:S(2)}) copy-start(bf16[128,640]{1,0:T(8,128)(2,1)} %param.7) | copy-start | bytes 491524
  4.9 0.6 copy-start.13
  7.3 1.6 copy-start.1
  47.6 2.4 %copy-start.3 = (bf16[1,4,4,48,8,24]{5,3,1,0,4,2:T(8,128)(2,1)S(1)}, bf16[1,4,4,48,8,24]{5,3,1,0,4,2:T(8,128)(2,1)}, u32[]{:S(2)}) copy-start(bf16[1,4,4,48,8,24]{5,3,1,0,4,2:T(8,128)(2,1)} %get-tuple-element.7) | copy-start | bytes 884740
  50.1 1.3 copy-start.7
  51.4 0.9 copy-start.9
  73.6 1.8 %copy-start.15 = (bf16[128,128]{1,0:T(8,128)(2,1)S(1)}, bf16[128,128]{1,0:T(8,128)(2,1)}, u32[]{:S(2)}) copy-start(bf16[128,128]{1,0:T(8,128)(2,1)} %param.8) | copy-start | bytes 98308
  75.5 2.2 %copy-start.10 = (f32[48,24,128]{2,1,0:T(8,128)S(1)}, f32[48,24,128]{2,1,0:T(8,128)}, u32[]{:S(2)}) copy-start(f32[48,24,128]{2,1,0:T(8,128)} %copy.77) | copy-start | bytes 1769476
  75.5 3.3 %copy-start.2 = (f32[48,24,640]{2,1,0:T(8,128)S(1)}, f32[48,24,640]{2,1,0:T(8,128)}, u32[]{:S(2)}) copy-start(f32[48,24,640]{2,1,0:T(8,128)} %copy-done.1) | copy-start | bytes 8847364
  77.7 1.1 copy-start.16
  106.5 4.7 %copy-start.8 = (bf16[4,192,192]{1,2,0:T(8,128)(2,1)S(1)}, bf16[4,192,192]{1,2,0:T(8,128)(2,1)}, u32[]{:S(2)}) copy-start(bf16[4,192,192]{1,2,0:T(8,128)(2,1)} %copy-done.7) | copy-start | bytes 884740
  179.3 1.4 copy-start.5
  179.3 1.7 copy-start.4
  181.0 1.1 copy-start.11
  181.0 1.1 copy-start.12
  181.3 1.1 copy-start.6
  181.3 1.1 copy-start.14

commit v2 on v1

v2 whole, which is shorter than its diff:
```python
import functools

import jax
import jax.numpy as jnp
from jax import lax
from jax.experimental import pallas as pl
from jax.experimental.pallas import tpu as pltpu
from jax.sharding import PartitionSpec as P

def normalize(values, axis):
    mean = jnp.mean(values, axis=axis, keepdims=True)
    centred = values - mean
    rstd = 1.0 / jnp.sqrt(jnp.mean(centred * centred, axis=axis, keepdims=True) + 1e-05)
    return (centred * rstd, rstd)


def norm_back(grad, normed, rstd, axis):
    return rstd * (
        grad
        - jnp.mean(grad, axis=axis, keepdims=True)
        - normed * jnp.mean(grad * normed, axis=axis, keepdims=True)
    )


def token_valid(positions, chain_tokens, slot):
    chain_of = positions // slot
    offset = positions - chain_of * slot
    onehot = chain_of[:, None] == jnp.arange(chain_tokens.shape[0], dtype=jnp.int32)[None, :]
    count = jnp.sum(jnp.where(onehot, chain_tokens[None, :], 0), axis=1)
    return (offset < count).astype(jnp.float32)


def exchange_kernel(rows, cols, src, dst, send_sem, recv_sem, own_sem):
    total = rows * cols
    me = lax.axis_index("row") * cols + lax.axis_index("col")
    barrier = pltpu.get_barrier_semaphore()

    def greet(step, carry):
        peer = lax.rem(me + step, total)
        pl.semaphore_signal(
            barrier,
            inc=1,
            device_id=(peer // cols, lax.rem(peer, cols)),
            device_id_type=pl.DeviceIdType.MESH,
        )
        return carry

    own = pltpu.make_async_copy(src.at[me], dst.at[me], own_sem)
    own.start()
    lax.fori_loop(1, total, greet, 0)
    pl.semaphore_wait(barrier, total - 1)

    def copy_to(step):
        peer = lax.rem(me + step, total)
        return pltpu.make_async_remote_copy(
            src_ref=src.at[peer],
            dst_ref=dst.at[me],
            send_sem=send_sem.at[peer],
            recv_sem=recv_sem.at[me],
            device_id=(peer // cols, lax.rem(peer, cols)),
            device_id_type=pl.DeviceIdType.MESH,
        )

    def copy_from(step):
        peer = lax.rem(me + step, total)
        return pltpu.make_async_remote_copy(
            src_ref=src.at[peer],
            dst_ref=dst.at[peer],
            send_sem=send_sem.at[peer],
            recv_sem=recv_sem.at[peer],
            device_id=(peer // cols, lax.rem(peer, cols)),
            device_id_type=pl.DeviceIdType.MESH,
        )

    def send(step, carry):
        copy_to(step).start()
        return carry

    def finish(step, carry):
        copy = copy_from(step)
        copy.wait_send()
        copy.wait_recv()
        return carry

    lax.fori_loop(1, total, send, 0)
    own.wait()
    lax.fori_loop(1, total, finish, 0)


def exchange(blocks, rows, cols, call):
    total = rows * cols
    return pl.pallas_call(
        functools.partial(exchange_kernel, rows, cols),
        out_shape=jax.ShapeDtypeStruct(blocks.shape, blocks.dtype),
        in_specs=[pl.BlockSpec(memory_space=pl.ANY)],
        out_specs=pl.BlockSpec(memory_space=pl.ANY),
        scratch_shapes=[
            pltpu.SemaphoreType.DMA((total,)),
            pltpu.SemaphoreType.DMA((total,)),
            pltpu.SemaphoreType.DMA,
        ],
        compiler_params=pltpu.CompilerParams(collective_id=call, has_side_effects=True),
        name="exchange",
    )(blocks)


def gather_plane(blocks, plane, channel, rows, cols, tile_i, tile_j):
    for r in range(rows):
        slab = jnp.concatenate(
            [
                blocks[r * cols + c].astype(jnp.float32)[channel : channel + 1]
                for c in range(cols)
            ],
            axis=0,
        )
        for t in range(tile_j):
            plane[t * cols : (t + 1) * cols, r * tile_i : (r + 1) * tile_i] = slab[
                :, t * tile_i : (t + 1) * tile_i
            ]


def scatter_plane(value, lines, channel, rows, cols, tile_i, tile_j):
    for r in range(rows):
        for t in range(tile_j):
            lines[r, channel, :, t * tile_i : (t + 1) * tile_i] = value[
                t * cols : (t + 1) * cols, r * tile_i : (r + 1) * tile_i
            ]


def write_blocks(lines, out, count, rows, cols):
    for r in range(rows):
        for c in range(cols):
            out[r * cols + c] = jnp.concatenate(
                [lines[r, n][c : c + 1] for n in range(count)], axis=0
            ).astype(jnp.bfloat16)


def natural_rows(tokens, cols, tile_j):
    row = lax.broadcasted_iota(jnp.int32, (tokens, tokens), 0)
    column = lax.broadcasted_iota(jnp.int32, (tokens, tokens), 1)
    wanted = lax.rem(row, tile_j) * cols + row // tile_j
    return jnp.where(column == wanted, 1.0, 0.0).astype(jnp.bfloat16)


def dot(a, b, dims):
    return lax.dot_general(a, b, (dims, ((), ())), preferred_element_type=jnp.float32)


def forward_kernel(sizes, own, blocks, out, planes, plane, lines):
    rows, cols, tile_i, tile_j = sizes
    order = natural_rows(rows * tile_i, cols, tile_j)
    for n in range(own):
        gather_plane(blocks, plane, n, *sizes)
        left = plane[...].astype(jnp.bfloat16)
        planes[n] = left
        gather_plane(blocks, plane, own + n, *sizes)
        right = plane[...].astype(jnp.bfloat16)
        planes[own + n] = right
        left = dot(order, left, ((1,), (0,))).astype(jnp.bfloat16)
        scatter_plane(dot(right, left, ((1,), (1,))), lines, n, *sizes)
    write_blocks(lines, out, own, rows, cols)


def backward_kernel(sizes, own, blocks, planes, out, plane, lines):
    rows, cols, tile_i, tile_j = sizes
    order = natural_rows(rows * tile_i, cols, tile_j)
    for n in range(own):
        gather_plane(blocks, plane, n, *sizes)
        grad = dot(plane[...].astype(jnp.bfloat16), order, ((1,), (0,))).astype(jnp.bfloat16)
        scatter_plane(dot(grad, planes[own + n], ((0,), (0,))), lines, n, *sizes)
        scatter_plane(dot(grad, planes[n], ((1,), (0,))), lines, own + n, *sizes)
    write_blocks(lines, out, 2 * own, rows, cols)


def on_device(pair, chain_tokens, w_in, w_out, grad_update):
    rows = lax.axis_size("row")
    cols = lax.axis_size("col")
    tile_i, tile_j, width = pair.shape
    tokens = tile_i * rows
    devices = rows * cols
    own = width // devices
    entries = tile_i * tile_j
    slot = tokens // chain_tokens.shape[0]
    sizes = (rows, cols, tile_i, tile_j)
    vmem = pl.BlockSpec(memory_space=pltpu.VMEM)

    def scratch(count):
        return [
            pltpu.VMEM((tokens, tokens), jnp.float32),
            pltpu.VMEM((rows, count, cols, entries), jnp.float32),
        ]

    params = pltpu.CompilerParams(vmem_limit_bytes=48 * 1024 * 1024)
    blocks_of = lambda count: jax.ShapeDtypeStruct((devices, count, entries), jnp.bfloat16)

    row_pos = lax.axis_index("row") * tile_i + jnp.arange(tile_i, dtype=jnp.int32)
    col_pos = lax.axis_index("col") * tile_j + jnp.arange(tile_j, dtype=jnp.int32)
    mask = (
        token_valid(col_pos, chain_tokens, slot)[:, None]
        * token_valid(row_pos, chain_tokens, slot)[None, :]
    ).reshape(1, entries)
    x = pair.transpose(1, 0, 2).reshape(entries, width).astype(jnp.float32)
    normed, rstd = normalize(x, 1)
    proj = dot(w_in, normed.astype(jnp.bfloat16), ((0,), (1,)))
    a_lin, a_gate, b_lin, b_gate, o_gate = (
        proj[n * width : (n + 1) * width] for n in range(5)
    )
    s_a = jax.nn.sigmoid(a_gate)
    s_b = jax.nn.sigmoid(b_gate)
    s_o = jax.nn.sigmoid(o_gate)
    left = (mask * s_a * a_lin).astype(jnp.bfloat16).reshape(devices, own, entries)
    right = (mask * s_b * b_lin).astype(jnp.bfloat16).reshape(devices, own, entries)
    moved = exchange(jnp.concatenate([left, right], axis=1), rows, cols, 0)
    outer, planes = pl.pallas_call(
        functools.partial(forward_kernel, sizes, own),
        out_shape=(
            blocks_of(own),
            jax.ShapeDtypeStruct((2 * own, tokens, tokens), jnp.bfloat16),
        ),
        in_specs=[vmem],
        out_specs=(vmem, vmem),
        scratch_shapes=scratch(own),
        compiler_params=params,
        name="outer",
    )(moved)
    outer = exchange(outer, rows, cols, 1).reshape(width, entries).astype(jnp.float32)
    onorm, orstd = normalize(outer, 0)
    value = dot(w_out, onorm.astype(jnp.bfloat16), ((0,), (0,)))
    grad32 = grad_update.transpose(1, 0, 2).reshape(entries, width).T.astype(jnp.float32)
    dvb = (grad32 * s_o).astype(jnp.bfloat16)
    du = dot(w_out, dvb, ((1,), (0,)))
    dob = norm_back(du, onorm, orstd, 0).astype(jnp.bfloat16)
    moved = exchange(dob.reshape(devices, own, entries), rows, cols, 2)
    grads = pl.pallas_call(
        functools.partial(backward_kernel, sizes, own),
        out_shape=blocks_of(2 * own),
        in_specs=[vmem, vmem],
        out_specs=vmem,
        scratch_shapes=scratch(2 * own),
        compiler_params=params,
        name="outer_back",
    )(moved, planes)
    update = (s_o * value).astype(jnp.bfloat16).T
    grads = exchange(grads, rows, cols, 3)
    d_left = grads[:, :own].reshape(width, entries).astype(jnp.float32) * mask
    d_right = grads[:, own:].reshape(width, entries).astype(jnp.float32) * mask
    dproj = jnp.concatenate(
        [
            d_left * s_a,
            d_left * a_lin * s_a * (1.0 - s_a),
            d_right * s_b,
            d_right * b_lin * s_b * (1.0 - s_b),
            grad32 * value * s_o * (1.0 - s_o),
        ],
        axis=0,
    ).astype(jnp.bfloat16)
    dx = dot(dproj, w_in, ((0,), (1,)))
    grad_pair = norm_back(dx, normed, rstd, 1).astype(jnp.bfloat16)

    def home(values):
        return values.reshape(tile_j, tile_i, width).transpose(1, 0, 2)

    return (home(update), home(grad_pair))


def solution(mesh):
    return jax.shard_map(
        on_device,
        mesh=mesh,
        in_specs=(P("row", "col", None), P(), P(), P(), P("row", "col", None)),
        out_specs=(P("row", "col", None), P("row", "col", None)),
        check_vma=False,
    )
```

time: 186 us -> 108 us (0.58)
  local copies, waits for them, and re-layouts: 87.6 us -> 16.1 us
  matrix products: 10.8 us -> 3.8 us
  Pallas kernels: 66.7 us -> 71.2 us
  other arithmetic: 18.5 us -> 15.2 us
    another operation x8 -> x0, local copies, waits for them, and re-layouts: 25.4 us -> none  [the longest x2 9.45 us: to_planes(): moved.reshape(rows, cols, count, own, tile_i, tile_j)]
    reshape x4, local copies, waits for them, and re-layouts: 20.6 us -> 1.73 us  [the longest x1 0.79 us: on_device(): moved = exchange(dob.reshape(devices, own, entries), rows, cols, 2)]
    convert_element_type x11 -> x5, local copies, waits for them, and re-layouts: 20 us -> 5.52 us  [the longest x1 2.1 us: on_device(): d_right = grads[:, own:].reshape(width, entries).astype(jnp.float32) * mask]
    transpose x5 -> x1, local copies, waits for them, and re-layouts: 12.8 us -> 0.21 us  [on_device(): update = (s_o * value).astype(jnp.bfloat16).T]
    dot_general x7 -> x4, matrix products: 10.8 us -> 3.8 us  [dot(): lax.dot_general(a, b, (dims, ((), ())), preferred_element_type=jnp.float32)]
    pallas_call x0 -> x2, Pallas kernels: none -> 5.99 us  [the longest x1 3.51 us: on_device(): pl.pallas_call(functools.partial(backward_kernel, sizes, own), out_shape=...]
    unnamed x34 -> x37, local copies, waits for them, and re-layouts: 2.75 us -> 8.19 us
    slice x3 -> x0, local copies, waits for them, and re-layouts: 5.28 us -> none  [on_device(): left_p, right_p = (planes[0], planes[1])]
where the time goes in v2:
time: 108 us; the launch traced here: 107 us
  Pallas kernels  71.2 us (66%)
  local copies, waits for them, and re-layouts  16.1 us (15%)
  other arithmetic  15.2 us (14%)
  matrix products  3.8 us (4%)
    pallas_call x4, Pallas kernels, exchange(): pl.pallas_call(functools.partial(exchange_kernel, rows, cols), out_shape=...  65.3 us
    unnamed x37, local copies, waits for them, and re-layouts  8.19 us
    dot_general x4, matrix products, dot(): lax.dot_general(a, b, (dims, ((), ())), preferred_element_type=jnp.float32)  3.8 us
    pallas_call x1, Pallas kernels, on_device(): pl.pallas_call(functools.partial(backward_kernel, sizes, own), out_shape=...  3.51 us
    convert_element_type x1, other arithmetic, on_device(): d_right = grads[:, own:].reshape(width, entries).astype(jnp.float32) * mask  2.62 us
    reduce_sum x2, other arithmetic, normalize(): jnp.mean(centred * centred, axis=axis, keepdims=True) + 1e-05  2.54 us
    pallas_call x1, Pallas kernels, on_device(): pl.pallas_call(functools.partial(forward_kernel, sizes, own), out_shape=(...  2.47 us
    reduce_sum x2, other arithmetic, normalize(): mean = jnp.mean(values, axis=axis, keepdims=True)  2.32 us

profile of v2, /device:TPU:15, one launch (start us, length us, event | category | flops | bytes accessed | tf_op | source)
XLA Modules:
  0.0 107.3 jit_solution(13585346384097342813)
XLA Ops:
  0.7 0.8 select_reduce_fusion.1
  1.5 0.7 select_reduce_fusion
  2.4 1.2 %fusion.26 = f32[24,48]{0,1:T(8,128)S(1)} fusion(bf16[48,24,128]{2,1,0:T(8,128)(2,1)} %param.5), kind=kLoop, calls=%fused_computation.49 | loop fusion | flops 293760 | bytes 299520 | tf_op jit(solution)/shard_map/reduce_sum | solution.py:11
  3.9 1.4 %multiply_reduce_fusion.2 = f32[24,48]{0,1:T(8,128)S(1)} fusion(bf16[48,24,128]{2,1,0:T(8,128)(2,1)} %param.5, f32[24,48]{0,1:T(8,128)S(1)} %copy.40), kind=kLoop, calls=%fused_computation.41 | loop fusion | flops 588672 | bytes 304128 | tf_op jit(solution)/shard_map/reduce_sum | solution.py:13
  5.4 1.0 copy_convert_fusion
  6.8 0.8 copy-done.7
  9.0 1.3 %copy-done.5 = f32[640,1152]{1,0:T(8,128)} copy-done((f32[640,1152]{1,0:T(8,128)}, f32[640,1152]{1,0:T(8,128)S(1)}, u32[]{:S(2)}) %copy-start.5) | copy-done | bytes 2949144
  10.4 1.1 %pad_maximum_fusion.src = bf16[32,8,1152]{2,1,0:T(8,128)(2,1)} fusion(bf16[32,4,1152]{2,1,0:T(4,128)(2,1)S(1)} %reshape.168, bf16[32,4,1152]{2,1,0:T(4,128)(2,1)S(1)} %reshape.167), kind=kLoop, calls=%fused_computation.14 | loop fusion | flops 1179648 | bytes 1179648 | tf_op jit(solution)/shard_map/concatenate | solution.py:213
  11.5 20.0 %exchange.4.blocks = bf16[32,8,1152]{2,1,0:T(8,128)(2,1)} custom-call(bf16[32,8,1152]{2,1,0:T(8,128)(2,1)} %pad_maximum_fusion.src), custom_call_target="tpu_custom_call" | custom-call | tf_op jit(solution)/shard_map/exchange/pallas_call | solution.py:92
  31.5 1.1 copy-done.2
  32.6 2.5 %outer.1 = (bf16[32,4,1152]{2,1,0:T(4,128)(2,1)S(1)}, bf16[8,192,192]{2,1,0:T(8,128)(2,1)S(1)}) custom-call(bf16[32,8,1152]{2,1,0:T(8,128)(2,1)S(1)} %copy-done.2), custom_call_target="tpu_custom_call" | custom-call | tf_op jit(solution)/shard_map/outer/pallas_call | solution.py:214
  35.1 0.7 copy-done.4
  35.8 13.0 %exchange.5 = bf16[32,4,1152]{2,1,0:T(4,128)(2,1)} custom-call(bf16[32,4,1152]{2,1,0:T(4,128)(2,1)} %copy-done.4), custom_call_target="tpu_custom_call" | custom-call | tf_op jit(solution)/shard_map/exchange/pallas_call | solution.py:92
  48.8 1.1 %convert_reduce_fusion = f32[1152]{0:T(1024)S(1)} fusion(bf16[32,4,1152]{2,1,0:T(4,128)(2,1)} %exchange.5), kind=kLoop, calls=%fused_computation.54 | loop fusion | flops 293760 | bytes 299520 | tf_op jit(solution)/shard_map/reduce_sum | solution.py:11
  49.9 1.2 %multiply_reduce_fusion.1 = f32[1152]{0:T(1024)S(1)} fusion(bf16[32,4,1152]{2,1,0:T(4,128)(2,1)} %exchange.5, f32[1152]{0:T(1024)S(1)} %broadcast_multiply_fusion.6), kind=kLoop, calls=%fused_computation.37 | loop fusion | flops 588672 | bytes 304128 | tf_op jit(solution)/shard_map/reduce_sum | solution.py:13
  51.1 1.0 reshape.173
  52.1 1.6 %fusion.12 = (f32[1152]{0:T(1024)S(1)}, f32[1152,128]{0,1:T(8,128)S(1)}) fusion(f32[128,1152]{1,0:T(8,128)S(1)} %reshape.173, f32[1152]{0:T(1024)S(1)} %add_rsqrt_fusion.1, f32[1152]{0:T(1024)S(1)} %broadcast_multiply_fusion.6, bf16[128,128]{1,0:T(8,128)(2,1)S(1)} %copy-done.17, f32[1152,128]{0,1:T(8,128)S(1)} %copy.45, f32[640,1152]{1,0:T(8,128)} %copy-done.5), kind=kOutput, calls=%fused_computation.20 | convolution fusion | flops 39074688 | bytes 2405888 | tf_op jit(solution)/shard_map/dot_general | solution.py:146
  53.9 0.8 reshape.170.src
  54.7 13.0 %exchange.6.blocks = bf16[32,4,1152]{2,1,0:T(4,128)(2,1)} custom-call(bf16[32,4,1152]{2,1,0:T(4,128)(2,1)} %reshape.170.src), custom_call_target="tpu_custom_call" | custom-call | tf_op jit(solution)/shard_map/exchange/pallas_call | solution.py:92
  67.8 1.0 copy-done.3
  68.7 3.5 %outer_back.1.src = bf16[32,8,1152]{2,1,0:T(8,128)(2,1)S(1)} custom-call(bf16[32,4,1152]{2,1,0:T(4,128)(2,1)S(1)} %copy-done.3, bf16[8,192,192]{2,1,0:T(8,128)(2,1)S(1)} %get-tuple-element.5.planes), custom_call_target="tpu_custom_call" | custom-call | tf_op jit(solution)/shard_map/outer_back/pallas_call | solution.py:234
  72.3 0.8 copy-done.1
  73.1 19.2 %exchange.7 = bf16[32,8,1152]{2,1,0:T(8,128)(2,1)} custom-call(bf16[32,8,1152]{2,1,0:T(8,128)(2,1)} %copy-done.1), custom_call_target="tpu_custom_call" | custom-call | tf_op jit(solution)/shard_map/exchange/pallas_call | solution.py:92
  92.3 2.6 %slice_convert_fusion = (f32[32,4,1152]{2,1,0:T(4,128)}, f32[32,4,1152]{2,1,0:T(4,128)}) fusion(bf16[32,8,1152]{2,1,0:T(8,128)(2,1)} %exchange.7), kind=kLoop, calls=%fused_computation.55 | loop fusion | flops 294912 | bytes 1769472 | tf_op jit(solution)/shard_map/convert_element_type | solution.py:246
  95.0 2.1 %reshape.175 = f32[128,1152]{1,0:T(8,128)} reshape(f32[32,4,1152]{2,1,0:T(4,128)} %get-tuple-element.18) | data formatting | bytes 1179648 | tf_op jit(solution)/shard_map/convert_element_type | solution.py:246
  97.1 2.1 %reshape.174 = f32[128,1152]{1,0:T(8,128)} reshape(f32[32,4,1152]{2,1,0:T(4,128)} %get-tuple-element.19) | data formatting | bytes 1179648 | tf_op jit(solution)/shard_map/convert_element_type | solution.py:245
  99.2 1.3 %fusion.22 = bf16[640,1152]{1,0:T(8,128)(2,1)S(1)} fusion(f32[128,1152]{1,0:T(8,128)} %reshape.174, f32[1152]{0:T(1024)S(1)} %mul.180, f32[640,1152]{1,0:T(8,128)S(1)} %copy-done.6), kind=kLoop, calls=%fused_computation.45 | loop fusion | flops 884735 | bytes 1479168
  102.5 0.9 copy-done.8
  103.4 1.2 %fusion.33 = (f32[1152]{0:T(1024)S(1)}, f32[1152]{0:T(1024)S(1)}, f32[1152,128]{1,0:T(8,128)S(1)}) fusion(f32[1152]{0:T(1024)S(1)} %sqrt.9, f32[1152]{0:T(1024)S(1)} %div.67, f32[24,48,128]{2,1,0:T(8,128)S(1)} %copy-done.8, bf16[640,1152]{1,0:T(8,128)(2,1)S(1)} %get-tuple-element.22, bf16[128,640]{1,0:T(8,128)(2,1)S(1)} %copy-done), kind=kOutput, calls=%fused_computation.78 | convolution fusion | flops 189478656 | bytes 2836480 | tf_op jit(solution)/shard_map/dot_general | solution.py:146
  104.8 0.8 copy.47
  105.6 0.9 multiply_convert_fusion
  106.5 0.8 copy.51
  (63 shorter events, 4.9 us)
Async XLA Ops:
  0.6 7.4 %copy-start = (bf16[128,640]{1,0:T(8,128)(2,1)S(1)}, bf16[128,640]{1,0:T(8,128)(2,1)}, u32[]{:S(2)}) copy-start(bf16[128,640]{1,0:T(8,128)(2,1)} %param.7) | copy-start | bytes 491524
  2.3 4.3 %copy-start.12 = (bf16[48,24,128]{2,1,0:T(8,128)(2,1)S(1)}, bf16[48,24,128]{2,1,0:T(8,128)(2,1)}, u32[]{:S(2)}) copy-start(bf16[48,24,128]{2,1,0:T(8,128)(2,1)} %param.5) | copy-start | bytes 884740
  6.6 45.4 %copy-start.15 = (f32[1152,128]{0,1:T(8,128)}, f32[1152,128]{0,1:T(8,128)S(1)}, u32[]{:S(2)}) copy-start(f32[1152,128]{0,1:T(8,128)S(1)} %copy.45) | copy-start | bytes 1769476
  6.8 0.8 copy-start.7
  8.6 1.6 %copy-start.5 = (f32[640,1152]{1,0:T(8,128)}, f32[640,1152]{1,0:T(8,128)S(1)}, u32[]{:S(2)}) copy-start(f32[640,1152]{1,0:T(8,128)S(1)} %convolution_bitcast_fusion) | copy-start | bytes 8847364
  31.5 1.1 copy-start.2
  32.6 19.5 %copy-start.17 = (bf16[128,128]{1,0:T(8,128)(2,1)S(1)}, bf16[128,128]{1,0:T(8,128)(2,1)}, u32[]{:S(2)}) copy-start(bf16[128,128]{1,0:T(8,128)(2,1)} %param.8) | copy-start | bytes 98308
  35.0 0.7 copy-start.4
  52.1 1.7 %copy-start.13 = (f32[128,1152]{1,0:T(8,128)}, f32[128,1152]{1,0:T(8,128)S(1)}, u32[]{:S(2)}) copy-start(f32[128,1152]{1,0:T(8,128)S(1)} %reshape.173) | copy-start | bytes 1769476
  67.8 1.0 copy-start.3
  72.3 0.8 copy-start.1
  92.3 6.8 %copy-start.6 = (f32[640,1152]{1,0:T(8,128)S(1)}, f32[640,1152]{1,0:T(8,128)}, u32[]{:S(2)}) copy-start(f32[640,1152]{1,0:T(8,128)} %copy-done.5) | copy-start | bytes 8847364
  99.2 1.3 %copy-start.11 = (f32[128,1152]{1,0:T(8,128)S(1)}, f32[128,1152]{1,0:T(8,128)}, u32[]{:S(2)}) copy-start(f32[128,1152]{1,0:T(8,128)} %reshape.174) | copy-start | bytes 1769476
  99.2 1.6 %copy-start.10 = (f32[128,1152]{1,0:T(8,128)S(1)}, f32[128,1152]{1,0:T(8,128)}, u32[]{:S(2)}) copy-start(f32[128,1152]{1,0:T(8,128)} %reshape.175) | copy-start | bytes 1769476
  100.7 1.1 copy-start.14
  100.7 1.2 %copy-start.16 = (f32[1152,128]{0,1:T(8,128)S(1)}, f32[1152,128]{0,1:T(8,128)}, u32[]{:S(2)}) copy-start(f32[1152,128]{0,1:T(8,128)} %copy-done.15) | copy-start | bytes 1769476
  102.3 1.1 copy-start.8
  103.4 2.3 %copy-start.9 = (f32[24,48,128]{2,1,0:T(8,128)S(1)}, f32[24,48,128]{2,1,0:T(8,128)}, u32[]{:S(2)}) copy-start(f32[24,48,128]{2,1,0:T(8,128)} %copy-done.7) | copy-start | bytes 1769476

commit v3 on v2

--- a/solution.py
+++ b/solution.py
@@ -30,7 +30,7 @@
     return (offset < count).astype(jnp.float32)
 
 
-def exchange_kernel(rows, cols, src, dst, send_sem, recv_sem, own_sem):
+def greet_all(rows, cols):
     total = rows * cols
     me = lax.axis_index("row") * cols + lax.axis_index("col")
     barrier = pltpu.get_barrier_semaphore()
@@ -45,63 +45,41 @@
         )
         return carry
 
-    own = pltpu.make_async_copy(src.at[me], dst.at[me], own_sem)
-    own.start()
     lax.fori_loop(1, total, greet, 0)
     pl.semaphore_wait(barrier, total - 1)
 
-    def copy_to(step):
+
+def exchange(rows, cols, src, dst, send_sem, recv_sem, own_sem):
+    total = rows * cols
+    me = lax.axis_index("row") * cols + lax.axis_index("col")
+
+    def copy(step, slot_of):
         peer = lax.rem(me + step, total)
+        slot = slot_of(peer)
         return pltpu.make_async_remote_copy(
             src_ref=src.at[peer],
-            dst_ref=dst.at[me],
+            dst_ref=dst.at[slot],
             send_sem=send_sem.at[peer],
-            recv_sem=recv_sem.at[me],
+            recv_sem=recv_sem.at[slot],
             device_id=(peer // cols, lax.rem(peer, cols)),
             device_id_type=pl.DeviceIdType.MESH,
         )
 
-    def copy_from(step):
-        peer = lax.rem(me + step, total)
-        return pltpu.make_async_remote_copy(
-            src_ref=src.at[peer],
-            dst_ref=dst.at[peer],
-            send_sem=send_sem.at[peer],
-            recv_sem=recv_sem.at[peer],
-            device_id=(peer // cols, lax.rem(peer, cols)),
-            device_id_type=pl.DeviceIdType.MESH,
-        )
-
     def send(step, carry):
-        copy_to(step).start()
+        copy(step, lambda peer: me).start()
         return carry
 
     def finish(step, carry):
-        copy = copy_from(step)
-        copy.wait_send()
-        copy.wait_recv()
+        pending = copy(step, lambda peer: peer)
+        pending.wait_send()
+        pending.wait_recv()
         return carry
 
+    own = pltpu.make_async_copy(src.at[me], dst.at[me], own_sem)
     lax.fori_loop(1, total, send, 0)
+    own.start()
     own.wait()
     lax.fori_loop(1, total, finish, 0)
-
-
-def exchange(blocks, rows, cols, call):
-    total = rows * cols
-    return pl.pallas_call(
-        functools.partial(exchange_kernel, rows, cols),
-        out_shape=jax.ShapeDtypeStruct(blocks.shape, blocks.dtype),
-        in_specs=[pl.BlockSpec(memory_space=pl.ANY)],
-        out_specs=pl.BlockSpec(memory_space=pl.ANY),
-        scratch_shapes=[
-            pltpu.SemaphoreType.DMA((total,)),
-            pltpu.SemaphoreType.DMA((total,)),
-            pltpu.SemaphoreType.DMA,
-        ],
-        compiler_params=pltpu.CompilerParams(collective_id=call, has_side_effects=True),
-        name="exchange",
-    )(blocks)
 
 
 def gather_plane(blocks, plane, channel, rows, cols, tile_i, tile_j):
@@ -172,6 +150,69 @@
     write_blocks(lines, out, 2 * own, rows, cols)
 
 
+def middle(own, total, received, gate, grad, w_out, update, d_gate, d_outer, chunk):
+    width, entries = gate.shape
+
+    def part(index, carry):
+        at = pl.ds(pl.multiple_of(index * chunk, chunk), chunk)
+        outer = jnp.concatenate(
+            [received[d, :, at].astype(jnp.float32) for d in range(total)], axis=0
+        )
+        s_o = gate[:, at]
+        grad32 = grad[:, at].astype(jnp.float32)
+        onorm, orstd = normalize(outer, 0)
+        value = dot(w_out[...], onorm.astype(jnp.bfloat16), ((0,), (0,)))
+        update[:, at] = (s_o * value).astype(jnp.bfloat16)
+        d_gate[:, at] = (grad32 * value * s_o * (1.0 - s_o)).astype(jnp.bfloat16)
+        du = dot(w_out[...], (grad32 * s_o).astype(jnp.bfloat16), ((1,), (0,)))
+        dob = norm_back(du, onorm, orstd, 0).astype(jnp.bfloat16)
+        for d in range(total):
+            d_outer[d, :, at] = dob[d * own : (d + 1) * own]
+        return carry
+
+    lax.fori_loop(0, entries // chunk, part, 0)
+
+
+def core_kernel(
+    sizes,
+    own,
+    sides,
+    gate,
+    grad,
+    w_out,
+    update,
+    d_gate,
+    grads,
+    sides_in,
+    outer_out,
+    outer_in,
+    d_outer,
+    d_outer_in,
+    grads_out,
+    planes,
+    plane,
+    lines,
+    send_sem,
+    recv_sem,
+    own_sem,
+):
+    rows, cols, tile_i, tile_j = sizes
+
+    def move(src, dst, phase):
+        exchange(
+            rows, cols, src, dst, send_sem.at[phase], recv_sem.at[phase], own_sem.at[phase]
+        )
+
+    greet_all(rows, cols)
+    move(sides, sides_in, 0)
+    forward_kernel(sizes, own, sides_in, outer_out, planes, plane, lines)
+    move(outer_out, outer_in, 1)
+    middle(own, rows * cols, outer_in, gate, grad, w_out, update, d_gate, d_outer, 128)
+    move(d_outer, d_outer_in, 2)
+    backward_kernel(sizes, own, d_outer_in, planes, grads_out, plane, lines)
+    move(grads_out, grads, 3)
+
+
 def on_device(pair, chain_tokens, w_in, w_out, grad_update):
     rows = lax.axis_size("row")
     cols = lax.axis_size("col")
@@ -184,14 +225,8 @@
     sizes = (rows, cols, tile_i, tile_j)
     vmem = pl.BlockSpec(memory_space=pltpu.VMEM)
 
-    def scratch(count):
-        return [
-            pltpu.VMEM((tokens, tokens), jnp.float32),
-            pltpu.VMEM((rows, count, cols, entries), jnp.float32),
-        ]
-
-    params = pltpu.CompilerParams(vmem_limit_bytes=48 * 1024 * 1024)
-    blocks_of = lambda count: jax.ShapeDtypeStruct((devices, count, entries), jnp.bfloat16)
+    whole = pl.BlockSpec(memory_space=pl.ANY)
+    block = lambda count: (devices, count, entries)
 
     row_pos = lax.axis_index("row") * tile_i + jnp.arange(tile_i, dtype=jnp.int32)
     col_pos = lax.axis_index("col") * tile_j + jnp.arange(tile_j, dtype=jnp.int32)
@@ -210,38 +245,34 @@
     s_o = jax.nn.sigmoid(o_gate)
     left = (mask * s_a * a_lin).astype(jnp.bfloat16).reshape(devices, own, entries)
     right = (mask * s_b * b_lin).astype(jnp.bfloat16).reshape(devices, own, entries)
-    moved = exchange(jnp.concatenate([left, right], axis=1), rows, cols, 0)
-    outer, planes = pl.pallas_call(
-        functools.partial(forward_kernel, sizes, own),
-        out_shape=(
-            blocks_of(own),
-            jax.ShapeDtypeStruct((2 * own, tokens, tokens), jnp.bfloat16),
+    sides = jnp.concatenate([left, right], axis=1)
+    grad_t = grad_update.transpose(1, 0, 2).reshape(entries, width).T
+    flat = jax.ShapeDtypeStruct((width, entries), jnp.bfloat16)
+    update, d_gate, grads = pl.pallas_call(
+        functools.partial(core_kernel, sizes, own),
+        out_shape=(flat, flat, jax.ShapeDtypeStruct(block(2 * own), jnp.bfloat16)),
+        in_specs=[vmem] * 4,
+        out_specs=(vmem, vmem, whole),
+        scratch_shapes=[
+            pltpu.VMEM(block(2 * own), jnp.bfloat16),
+            pltpu.VMEM(block(own), jnp.bfloat16),
+            pltpu.VMEM(block(own), jnp.bfloat16),
+            pltpu.VMEM(block(own), jnp.bfloat16),
+            pltpu.VMEM(block(own), jnp.bfloat16),
+            pltpu.VMEM(block(2 * own), jnp.bfloat16),
+            pltpu.VMEM((2 * own, tokens, tokens), jnp.bfloat16),
+            pltpu.VMEM((tokens, tokens), jnp.float32),
+            pltpu.VMEM((rows, 2 * own, cols, entries), jnp.float32),
+            pltpu.SemaphoreType.DMA((4, devices)),
+            pltpu.SemaphoreType.DMA((4, devices)),
+            pltpu.SemaphoreType.DMA((4,)),
+        ],
+        compiler_params=pltpu.CompilerParams(
+            collective_id=0, has_side_effects=True, vmem_limit_bytes=56 * 1024 * 1024
         ),
-        in_specs=[vmem],
-        out_specs=(vmem, vmem),
-        scratch_shapes=scratch(own),
-        compiler_params=params,
-        name="outer",
-    )(moved)
-    outer = exchange(outer, rows, cols, 1).reshape(width, entries).astype(jnp.float32)
-    onorm, orstd = normalize(outer, 0)
-    value = dot(w_out, onorm.astype(jnp.bfloat16), ((0,), (0,)))
-    grad32 = grad_update.transpose(1, 0, 2).reshape(entries, width).T.astype(jnp.float32)
-    dvb = (grad32 * s_o).astype(jnp.bfloat16)
-    du = dot(w_out, dvb, ((1,), (0,)))
-    dob = norm_back(du, onorm, orstd, 0).astype(jnp.bfloat16)
-    moved = exchange(dob.reshape(devices, own, entries), rows, cols, 2)
-    grads = pl.pallas_call(
-        functools.partial(backward_kernel, sizes, own),
-        out_shape=blocks_of(2 * own),
-        in_specs=[vmem, vmem],
-        out_specs=vmem,
-        scratch_shapes=scratch(2 * own),
-        compiler_params=params,
-        name="outer_back",
-    )(moved, planes)
-    update = (s_o * value).astype(jnp.bfloat16).T
-    grads = exchange(grads, rows, cols, 3)
+        name="core",
+    )(sides, s_o, grad_t, w_out)
+    update = update.T
     d_left = grads[:, :own].reshape(width, entries).astype(jnp.float32) * mask
     d_right = grads[:, own:].reshape(width, entries).astype(jnp.float32) * mask
     dproj = jnp.concatenate(
@@ -250,10 +281,10 @@
             d_left * a_lin * s_a * (1.0 - s_a),
             d_right * s_b,
             d_right * b_lin * s_b * (1.0 - s_b),
-            grad32 * value * s_o * (1.0 - s_o),
         ],
         axis=0,
     ).astype(jnp.bfloat16)
+    dproj = jnp.concatenate([dproj, d_gate], axis=0)
     dx = dot(dproj, w_in, ((0,), (1,)))
     grad_pair = norm_back(dx, normed, rstd, 1).astype(jnp.bfloat16)
 

time: 108 us -> 93.9 us (0.87)
  Pallas kernels: 71.2 us -> 63.1 us
  local copies, waits for them, and re-layouts: 16.1 us -> 13.6 us
  matrix products: 3.8 us -> 1.81 us
  other arithmetic: 15.2 us -> 13.6 us
    pallas_call x6 -> x1, Pallas kernels: 71.2 us -> 63.1 us  [on_device(): pl.pallas_call(functools.partial(core_kernel, sizes, own), out_shape=(fla...]
    unnamed x37 -> x16, local copies, waits for them, and re-layouts: 8.19 us -> 3.48 us
    dot_general x4 -> x2, matrix products: 3.8 us -> 1.81 us  [dot(): lax.dot_general(a, b, (dims, ((), ())), preferred_element_type=jnp.float32)]
    reshape x1, local copies, waits for them, and re-layouts: 0.07 us -> 1.75 us  [on_device(): (mask * s_a * a_lin).astype(jnp.bfloat16).reshape(devices, own, entries)]
    convert_element_type x2 -> x0, local copies, waits for them, and re-layouts: 1.23 us -> none  [the longest x1 1 us: on_device(): exchange(outer, rows, cols, 1).reshape(width, entries).astype(jnp.float32)]
    reduce_sum x2 -> x1, other arithmetic: 2.54 us -> 1.36 us  [normalize(): jnp.mean(centred * centred, axis=axis, keepdims=True) + 1e-05]
    convert_element_type x2 -> x0, other arithmetic: 1.15 us -> none  [the longest x1 1.01 us: on_device(): grad_update.transpose(1, 0, 2).reshape(entries, width).T.astype(jnp.float32)]
    reduce_sum x2 -> x1, other arithmetic: 2.32 us -> 1.19 us  [normalize(): mean = jnp.mean(values, axis=axis, keepdims=True)]
where the time goes in v3:
time: 93.9 us; the launch traced here: 92.9 us
  Pallas kernels  63.1 us (67%)
  local copies, waits for them, and re-layouts  13.6 us (14%)
  other arithmetic  13.6 us (14%)
  matrix products  1.81 us (2%)
    pallas_call x1, Pallas kernels, on_device(): pl.pallas_call(functools.partial(core_kernel, sizes, own), out_shape=(fla...  63.1 us
    unnamed x16, local copies, waits for them, and re-layouts  3.48 us
    convert_element_type x1, other arithmetic, on_device(): d_right = grads[:, own:].reshape(width, entries).astype(jnp.float32) * mask  2.5 us
    concatenate x1, other arithmetic, on_device(): sides = jnp.concatenate([left, right], axis=1)  2.17 us
    convert_element_type x1, local copies, waits for them, and re-layouts, on_device(): d_left = grads[:, :own].reshape(width, entries).astype(jnp.float32) * mask  2.1 us
    convert_element_type x1, local copies, waits for them, and re-layouts, on_device(): d_right = grads[:, own:].reshape(width, entries).astype(jnp.float32) * mask  2.08 us
    unnamed x4, other arithmetic  1.93 us

profile of v3, /device:TPU:15, one launch (start us, length us, event | category | flops | bytes accessed | tf_op | source)
XLA Modules:
  0.0 92.9 jit_solution(5372811575374825356)
XLA Ops:
  0.7 0.8 select_reduce_fusion.1
  1.5 0.7 select_reduce_fusion
  2.4 0.1 mul.133
  2.4 1.2 %fusion.15 = f32[24,48]{0,1:T(8,128)S(1)} fusion(bf16[48,24,128]{2,1,0:T(8,128)(2,1)} %param.5), kind=kLoop, calls=%fused_computation.31 | loop fusion | flops 293760 | bytes 299520 | tf_op jit(solution)/shard_map/reduce_sum | solution.py:11
  3.8 0.1 copy.36
  3.9 1.4 %multiply_reduce_fusion.1 = f32[24,48]{0,1:T(8,128)S(1)} fusion(bf16[48,24,128]{2,1,0:T(8,128)(2,1)} %param.5, f32[24,48]{0,1:T(8,128)S(1)} %copy.36), kind=kLoop, calls=%fused_computation.25 | loop fusion | flops 588672 | bytes 304128 | tf_op jit(solution)/shard_map/reduce_sum | solution.py:13
  5.3 0.1 sqrt.6
  5.4 1.0 %copy.38 = bf16[48,24,128]{2,0,1:T(8,128)(2,1)S(1)} copy(bf16[48,24,128]{2,1,0:T(8,128)(2,1)} %param.9) | data formatting | bytes 589824 | tf_op args[4]
  6.4 0.9 copy.39
  7.3 0.1 copy.34
  7.5 0.8 copy-done.1
  8.3 0.4 fusion.10
  8.7 0.6 convolution_bitcast_fusion
  9.3 1.4 %multiply_convert_fusion.6 = (bf16[128,1152]{1,0:T(8,128)(2,1)}, bf16[128,1152]{1,0:T(8,128)(2,1)S(1)}, f32[128,1152]{1,0:T(8,128)}) fusion(f32[640,1152]{1,0:T(8,128)S(1)} %convolution_bitcast_fusion, f32[1152]{0:T(1024)S(1)} %mul.133), kind=kLoop, calls=%fused_computation.24 | loop fusion | flops 2211840 | bytes 4133376 | tf_op jit(solution)/shard_map/convert_element_type | solution.py:246
  10.6 1.8 %reshape.135 = bf16[32,4,1152]{2,1,0:T(4,128)(2,1)} reshape(bf16[128,1152]{1,0:T(8,128)(2,1)} %get-tuple-element.18) | data formatting | bytes 589824 | tf_op jit(solution)/shard_map/reshape | solution.py:246
  12.4 0.8 reshape.136
  13.2 2.2 %pad_maximum_fusion.sides = bf16[32,8,1152]{2,1,0:T(8,128)(2,1)} fusion(bf16[32,4,1152]{2,1,0:T(4,128)(2,1)} %reshape.136, bf16[32,4,1152]{2,1,0:T(4,128)(2,1)} %reshape.135), kind=kLoop, calls=%fused_computation.13 | loop fusion | flops 1179648 | bytes 1179648 | tf_op jit(solution)/shard_map/concatenate | solution.py:248
  15.4 63.1 %core.1 = (bf16[128,1152]{1,0:T(8,128)(2,1)}, bf16[128,1152]{1,0:T(8,128)(2,1)}, bf16[32,8,1152]{2,1,0:T(8,128)(2,1)}) custom-call(bf16[32,8,1152]{2,1,0:T(8,128)(2,1)} %pad_maximum_fusion.sides, f32[128,1152]{1,0:T(8,128)} %get-tuple-element.20.gate, bf16[128,1152]{1,0:T(8,128)(2,1)} %bitcast.36, bf16[128,128]{1,0:T(8,128)(2,1)} %w_out.1), custom_call_target="tpu_custom_call" | custom-call | tf_op jit(solution)/shard_map/core/pallas_call | solution.py:251
  78.5 1.2 %copy.40 = bf16[1152,128]{1,0:T(8,128)(2,1)S(1)} copy(bf16[1152,128]{0,1:T(8,128)(2,1)} %bitcast.39) | data formatting | bytes 589824 | tf_op jit(solution)/shard_map/transpose | solution.py:275
  79.6 0.8 copy.42
  80.4 2.5 %slice_convert_fusion = (f32[32,4,1152]{2,1,0:T(4,128)}, f32[32,4,1152]{2,1,0:T(4,128)}) fusion(bf16[32,8,1152]{2,1,0:T(8,128)(2,1)} %get-tuple-element.6), kind=kLoop, calls=%fused_computation.33 | loop fusion | flops 294912 | bytes 1769472 | tf_op jit(solution)/shard_map/convert_element_type | solution.py:277
  82.9 2.1 %reshape.142 = f32[128,1152]{1,0:T(8,128)} reshape(f32[32,4,1152]{2,1,0:T(4,128)} %get-tuple-element.21) | data formatting | bytes 1179648 | tf_op jit(solution)/shard_map/convert_element_type | solution.py:277
  85.0 2.1 %reshape.141 = f32[128,1152]{1,0:T(8,128)} reshape(f32[32,4,1152]{2,1,0:T(4,128)} %get-tuple-element.22) | data formatting | bytes 1179648 | tf_op jit(solution)/shard_map/convert_element_type | solution.py:276
  87.1 1.3 %fusion.11 = bf16[640,1152]{1,0:T(8,128)(2,1)S(1)} fusion(f32[128,1152]{1,0:T(8,128)} %reshape.141, f32[1152]{0:T(1024)S(1)} %mul.133, f32[640,1152]{1,0:T(8,128)S(1)} %convolution_bitcast_fusion), kind=kLoop, calls=%fused_computation.27 | loop fusion | flops 884735 | bytes 1479168
  88.4 0.2 fusion.12
  88.7 0.2 fusion.13
  88.9 0.2 fusion.14
  89.1 0.5 copy-done.6
  89.6 0.3 copy-done.2
  89.9 1.2 %fusion.16 = (f32[1152]{0:T(1024)S(1)}, f32[1152]{0:T(1024)S(1)}, f32[1152,128]{1,0:T(8,128)S(1)}) fusion(f32[1152]{0:T(1024)S(1)} %sqrt.6, f32[1152]{0:T(1024)S(1)} %div.55, f32[24,48,128]{2,1,0:T(8,128)S(1)} %copy-done.2, bf16[640,1152]{1,0:T(8,128)(2,1)S(1)} %constant_dynamic-update-slice_fusion, bf16[128,640]{1,0:T(8,128)(2,1)S(1)} %copy-done), kind=kOutput, calls=%fused_computation.51 | convolution fusion | flops 189478656 | bytes 2836480 | tf_op jit(solution)/shard_map/dot_general | solution.py:124
  91.2 0.9 %multiply_convert_fusion = bf16[1152,128]{1,0:T(8,128)(2,1)S(1)} fusion(f32[1152,128]{1,0:T(8,128)S(1)} %get-tuple-element.23, f32[24,48,128]{2,1,0:T(8,128)S(1)} %copy-done.2, f32[1152]{0:T(1024)S(1)} %get-tuple-element.24, f32[1152]{0:T(1024)S(1)} %get-tuple-element.25, f32[1152]{0:T(1024)S(1)} %sqrt.6, f32[1152]{0:T(1024)S(1)} %div.55), kind=kLoop, calls=%fused_computation.17 | loop fusion | flops 1032192 | bytes 1492992 | tf_op jit(solution)/shard_map/convert_element_type | solution.py:289
  92.1 0.8 copy.44
  (24 shorter events, 0.5 us)
Async XLA Ops:
  0.6 8.0 %copy-start = (bf16[128,640]{1,0:T(8,128)(2,1)S(1)}, bf16[128,640]{1,0:T(8,128)(2,1)}, u32[]{:S(2)}) copy-start(bf16[128,640]{1,0:T(8,128)(2,1)} %param.7) | copy-start | bytes 491524
  0.6 6.7 %copy-start.5 = (bf16[48,24,128]{2,1,0:T(8,128)(2,1)S(1)}, bf16[48,24,128]{2,1,0:T(8,128)(2,1)}, u32[]{:S(2)}) copy-start(bf16[48,24,128]{2,1,0:T(8,128)(2,1)} %param.5) | copy-start | bytes 884740
  7.5 0.8 copy-start.1
  87.1 1.3 %copy-start.4 = (f32[128,1152]{1,0:T(8,128)S(1)}, f32[128,1152]{1,0:T(8,128)}, u32[]{:S(2)}) copy-start(f32[128,1152]{1,0:T(8,128)} %reshape.141) | copy-start | bytes 1769476
  87.1 1.6 %copy-start.3 = (f32[128,1152]{1,0:T(8,128)S(1)}, f32[128,1152]{1,0:T(8,128)}, u32[]{:S(2)}) copy-start(f32[128,1152]{1,0:T(8,128)} %reshape.142) | copy-start | bytes 1769476
  88.7 1.0 %copy-start.6 = (bf16[128,1152]{1,0:T(8,128)(2,1)S(1)}, bf16[128,1152]{1,0:T(8,128)(2,1)}, u32[]{:S(2)}) copy-start(bf16[128,1152]{1,0:T(8,128)(2,1)} %get-tuple-element.7) | copy-start | bytes 884740
  88.9 1.1 %copy-start.2 = (f32[24,48,128]{2,1,0:T(8,128)S(1)}, f32[24,48,128]{2,1,0:T(8,128)}, u32[]{:S(2)}) copy-start(f32[24,48,128]{2,1,0:T(8,128)} %copy-done.1) | copy-start | bytes 1769476

commit v4 on v3

--- a/solution.py
+++ b/solution.py
@@ -150,19 +150,40 @@
     write_blocks(lines, out, 2 * own, rows, cols)
 
 
-def middle(own, total, received, gate, grad, w_out, update, d_gate, d_outer, chunk):
-    width, entries = gate.shape
+def first(own, total, x, mask, w_in, proj, sides, chunk):
+    entries, width = x.shape
+
+    def part(index, carry):
+        at = pl.ds(pl.multiple_of(index * chunk, chunk), chunk)
+        normed, _ = normalize(x[at, :].astype(jnp.float32), 1)
+        lines = dot(w_in[...], normed.astype(jnp.bfloat16), ((0,), (1,)))
+        proj[:, at] = lines
+        a_lin, a_gate, b_lin, b_gate = (lines[n * width : (n + 1) * width] for n in range(4))
+        left = mask[:, at] * jax.nn.sigmoid(a_gate) * a_lin
+        right = mask[:, at] * jax.nn.sigmoid(b_gate) * b_lin
+        for d in range(total):
+            own_rows = slice(d * own, (d + 1) * own)
+            sides[d, :, at] = jnp.concatenate([left[own_rows], right[own_rows]], axis=0).astype(
+                jnp.bfloat16
+            )
+        return carry
+
+    lax.fori_loop(0, entries // chunk, part, 0)
+
+
+def middle(own, total, received, proj, grad, w_out, update, d_gate, d_outer, chunk):
+    entries, width = grad.shape
 
     def part(index, carry):
         at = pl.ds(pl.multiple_of(index * chunk, chunk), chunk)
         outer = jnp.concatenate(
             [received[d, :, at].astype(jnp.float32) for d in range(total)], axis=0
         )
-        s_o = gate[:, at]
-        grad32 = grad[:, at].astype(jnp.float32)
+        s_o = jax.nn.sigmoid(proj[4 * width : 5 * width, at])
+        grad32 = grad[at, :].astype(jnp.float32).T
         onorm, orstd = normalize(outer, 0)
         value = dot(w_out[...], onorm.astype(jnp.bfloat16), ((0,), (0,)))
-        update[:, at] = (s_o * value).astype(jnp.bfloat16)
+        update[at, :] = (s_o * value).T.astype(jnp.bfloat16)
         d_gate[:, at] = (grad32 * value * s_o * (1.0 - s_o)).astype(jnp.bfloat16)
         du = dot(w_out[...], (grad32 * s_o).astype(jnp.bfloat16), ((1,), (0,)))
         dob = norm_back(du, onorm, orstd, 0).astype(jnp.bfloat16)
@@ -173,22 +194,54 @@
     lax.fori_loop(0, entries // chunk, part, 0)
 
 
+def last(own, total, x, mask, w_in, proj, grads, d_gate, grad_pair, chunk):
+    entries, width = x.shape
+
+    def part(index, carry):
+        at = pl.ds(pl.multiple_of(index * chunk, chunk), chunk)
+        arrived = [grads[d, :, at].astype(jnp.float32) for d in range(total)]
+        d_left = jnp.concatenate([block[:own] for block in arrived], axis=0) * mask[:, at]
+        d_right = jnp.concatenate([block[own:] for block in arrived], axis=0) * mask[:, at]
+        a_lin, a_gate, b_lin, b_gate = (
+            proj[n * width : (n + 1) * width, at] for n in range(4)
+        )
+        s_a = jax.nn.sigmoid(a_gate)
+        s_b = jax.nn.sigmoid(b_gate)
+        parts = [
+            d_left * s_a,
+            d_left * a_lin * s_a * (1.0 - s_a),
+            d_right * s_b,
+            d_right * b_lin * s_b * (1.0 - s_b),
+        ]
+        dproj = jnp.concatenate([p.astype(jnp.bfloat16) for p in parts] + [d_gate[:, at]], axis=0)
+        dx = dot(dproj, w_in[...], ((0,), (1,)))
+        normed, rstd = normalize(x[at, :].astype(jnp.float32), 1)
+        grad_pair[at, :] = norm_back(dx, normed, rstd, 1).astype(jnp.bfloat16)
+        return carry
+
+    lax.fori_loop(0, entries // chunk, part, 0)
+
+
 def core_kernel(
     sizes,
     own,
+    x,
+    mask,
+    w_in,
+    w_out,
+    grad,
+    update,
+    grad_pair,
+    proj,
+    d_gate,
     sides,
-    gate,
-    grad,
-    w_out,
-    update,
-    d_gate,
-    grads,
     sides_in,
     outer_out,
     outer_in,
     d_outer,
     d_outer_in,
     grads_out,
+    grads,
     planes,
     plane,
     lines,
@@ -197,20 +250,23 @@
     own_sem,
 ):
     rows, cols, tile_i, tile_j = sizes
+    total = rows * cols
 
     def move(src, dst, phase):
         exchange(
             rows, cols, src, dst, send_sem.at[phase], recv_sem.at[phase], own_sem.at[phase]
         )
 
+    first(own, total, x, mask, w_in, proj, sides, 128)
     greet_all(rows, cols)
     move(sides, sides_in, 0)
     forward_kernel(sizes, own, sides_in, outer_out, planes, plane, lines)
     move(outer_out, outer_in, 1)
-    middle(own, rows * cols, outer_in, gate, grad, w_out, update, d_gate, d_outer, 128)
+    middle(own, total, outer_in, proj, grad, w_out, update, d_gate, d_outer, 128)
     move(d_outer, d_outer_in, 2)
     backward_kernel(sizes, own, d_outer_in, planes, grads_out, plane, lines)
     move(grads_out, grads, 3)
+    last(own, total, x, mask, w_in, proj, grads, d_gate, grad_pair, 128)
 
 
 def on_device(pair, chain_tokens, w_in, w_out, grad_update):
@@ -224,9 +280,7 @@
     slot = tokens // chain_tokens.shape[0]
     sizes = (rows, cols, tile_i, tile_j)
     vmem = pl.BlockSpec(memory_space=pltpu.VMEM)
-
-    whole = pl.BlockSpec(memory_space=pl.ANY)
-    block = lambda count: (devices, count, entries)
+    block = lambda count: pltpu.VMEM((devices, count, entries), jnp.bfloat16)
 
     row_pos = lax.axis_index("row") * tile_i + jnp.arange(tile_i, dtype=jnp.int32)
     col_pos = lax.axis_index("col") * tile_j + jnp.arange(tile_j, dtype=jnp.int32)
@@ -234,32 +288,30 @@
         token_valid(col_pos, chain_tokens, slot)[:, None]
         * token_valid(row_pos, chain_tokens, slot)[None, :]
     ).reshape(1, entries)
-    x = pair.transpose(1, 0, 2).reshape(entries, width).astype(jnp.float32)
-    normed, rstd = normalize(x, 1)
-    proj = dot(w_in, normed.astype(jnp.bfloat16), ((0,), (1,)))
-    a_lin, a_gate, b_lin, b_gate, o_gate = (
-        proj[n * width : (n + 1) * width] for n in range(5)
-    )
-    s_a = jax.nn.sigmoid(a_gate)
-    s_b = jax.nn.sigmoid(b_gate)
-    s_o = jax.nn.sigmoid(o_gate)
-    left = (mask * s_a * a_lin).astype(jnp.bfloat16).reshape(devices, own, entries)
-    right = (mask * s_b * b_lin).astype(jnp.bfloat16).reshape(devices, own, entries)
-    sides = jnp.concatenate([left, right], axis=1)
-    grad_t = grad_update.transpose(1, 0, 2).reshape(entries, width).T
-    flat = jax.ShapeDtypeStruct((width, entries), jnp.bfloat16)
-    update, d_gate, grads = pl.pallas_call(
+
+    def turned(values):
+        return values.transpose(1, 0, 2).reshape(entries, width)
+
+    def home(values):
+        return values.reshape(tile_j, tile_i, width).transpose(1, 0, 2)
+
+    flat = jax.ShapeDtypeStruct((entries, width), jnp.bfloat16)
+    update, grad_pair = pl.pallas_call(
         functools.partial(core_kernel, sizes, own),
-        out_shape=(flat, flat, jax.ShapeDtypeStruct(block(2 * own), jnp.bfloat16)),
-        in_specs=[vmem] * 4,
-        out_specs=(vmem, vmem, whole),
+        out_shape=(flat, flat),
+        in_specs=[vmem] * 5,
+        out_specs=(vmem, vmem),
         scratch_shapes=[
-            pltpu.VMEM(block(2 * own), jnp.bfloat16),
-            pltpu.VMEM(block(own), jnp.bfloat16),
-            pltpu.VMEM(block(own), jnp.bfloat16),
-            pltpu.VMEM(block(own), jnp.bfloat16),
-            pltpu.VMEM(block(own), jnp.bfloat16),
-            pltpu.VMEM(block(2 * own), jnp.bfloat16),
+            pltpu.VMEM((5 * width, entries), jnp.float32),
+            pltpu.VMEM((width, entries), jnp.bfloat16),
+            block(2 * own),
+            block(2 * own),
+            block(own),
+            block(own),
+            block(own),
+            block(own),
+            block(2 * own),
+            block(2 * own),
             pltpu.VMEM((2 * own, tokens, tokens), jnp.bfloat16),
             pltpu.VMEM((tokens, tokens), jnp.float32),
             pltpu.VMEM((rows, 2 * own, cols, entries), jnp.float32),
@@ -271,26 +323,7 @@
             collective_id=0, has_side_effects=True, vmem_limit_bytes=56 * 1024 * 1024
         ),
         name="core",
-    )(sides, s_o, grad_t, w_out)
-    update = update.T
-    d_left = grads[:, :own].reshape(width, entries).astype(jnp.float32) * mask
-    d_right = grads[:, own:].reshape(width, entries).astype(jnp.float32) * mask
-    dproj = jnp.concatenate(
-        [
-            d_left * s_a,
-            d_left * a_lin * s_a * (1.0 - s_a),
-            d_right * s_b,
-            d_right * b_lin * s_b * (1.0 - s_b),
-        ],
-        axis=0,
-    ).astype(jnp.bfloat16)
-    dproj = jnp.concatenate([dproj, d_gate], axis=0)
-    dx = dot(dproj, w_in, ((0,), (1,)))
-    grad_pair = norm_back(dx, normed, rstd, 1).astype(jnp.bfloat16)
-
-    def home(values):
-        return values.reshape(tile_j, tile_i, width).transpose(1, 0, 2)
-
+    )(turned(pair), mask, w_in, w_out, turned(grad_update))
     return (home(update), home(grad_pair))
 
 

time: 93.9 us -> 78.1 us (0.83)
  other arithmetic: 13.6 us -> 0.31 us
  local copies, waits for them, and re-layouts: 13.6 us -> 5.84 us
  Pallas kernels: 63.1 us -> 70.7 us
  matrix products: 1.81 us -> 0 us
    pallas_call x1, Pallas kernels: 63.1 us -> 70.7 us  [on_device(): pl.pallas_call(functools.partial(core_kernel, sizes, own), out_shape=(fla...]
    convert_element_type x5 -> x0, other arithmetic: 5.23 us -> none  [the longest x1 2.5 us: on_device(): d_right = grads[:, own:].reshape(width, entries).astype(jnp.float32) * mask]
    convert_element_type x3 -> x0, local copies, waits for them, and re-layouts: 4.29 us -> none  [the longest x1 2.1 us: on_device(): d_left = grads[:, :own].reshape(width, entries).astype(jnp.float32) * mask]
    reshape x4 -> x0, local copies, waits for them, and re-layouts: 4.22 us -> none  [the longest x1 1.75 us: on_device(): (mask * s_a * a_lin).astype(jnp.bfloat16).reshape(devices, own, entries)]
    transpose x1 -> x3, local copies, waits for them, and re-layouts: 1.17 us -> 4.53 us  [the longest x2 2.51 us: turned(): return values.transpose(1, 0, 2).reshape(entries, width)]
    unnamed x16 -> x4, local copies, waits for them, and re-layouts: 3.48 us -> 0.63 us
    reduce_sum x2 -> x0, other arithmetic: 2.55 us -> none  [the longest x1 1.36 us: normalize(): jnp.mean(centred * centred, axis=axis, keepdims=True) + 1e-05]
    concatenate x1 -> x0, other arithmetic: 2.17 us -> none  [on_device(): sides = jnp.concatenate([left, right], axis=1)]
where the time goes in v4:
time: 78.1 us; the launch traced here: 77.6 us
  Pallas kernels  70.7 us (91%)
  local copies, waits for them, and re-layouts  5.84 us (7%)
    pallas_call x1, Pallas kernels, on_device(): pl.pallas_call(functools.partial(core_kernel, sizes, own), out_shape=(fla...  70.7 us
    transpose x2, local copies, waits for them, and re-layouts, turned(): return values.transpose(1, 0, 2).reshape(entries, width)  2.51 us
    transpose x1, local copies, waits for them, and re-layouts, home(): return values.reshape(tile_j, tile_i, width).transpose(1, 0, 2)  2.01 us

profile of v4, /device:TPU:15, one launch (start us, length us, event | category | flops | bytes accessed | tf_op | source)
XLA Modules:
  0.0 77.6 jit_solution(10448810414947808997)
XLA Ops:
  0.6 0.0 copy-start.1
  0.7 0.6 copy-done.1
  1.3 0.1 select_reduce_fusion.1
  1.4 0.1 select_reduce_fusion
  1.5 0.1 broadcast_multiply_fusion
  1.6 0.7 mul.51.mask
  2.3 0.0 copy-start
  2.3 1.8 %copy.11 = bf16[24,48,128]{2,1,0:T(8,128)(2,1)} copy(bf16[24,48,128]{2,0,1:T(8,128)(2,1)} %bitcast.12) | data formatting | bytes 589824 | tf_op jit(solution)/shard_map/transpose | solution.py:293
  4.0 0.0 copy-done
  4.0 0.8 copy.12
  4.8 70.7 %core.1 = (bf16[1152,128]{1,0:T(8,128)(2,1)}, bf16[1152,128]{1,0:T(8,128)(2,1)}) custom-call(bf16[1152,128]{1,0:T(8,128)(2,1)} %bitcast.10, f32[1,1152]{1,0:T(1,128)} %mul.51.mask, bf16[128,640]{1,0:T(8,128)(2,1)} %w_in.1, bf16[128,128]{1,0:T(8,128)(2,1)} %w_out.1, bf16[1152,128]{1,0:T(8,128)(2,1)} %bitcast.11), custom_call_target="tpu_custom_call" | custom-call | tf_op jit(solution)/shard_map/core/pallas_call | solution.py:299
  75.5 2.0 %copy_bitcast_fusion = (bf16[48,24,128]{2,1,0:T(8,128)(2,1)}, bf16[48,24,128]{2,1,0:T(8,128)(2,1)}) fusion(bf16[24,48,128]{2,1,0:T(8,128)(2,1)} %bitcast.15, bf16[24,48,128]{2,1,0:T(8,128)(2,1)} %bitcast.14), kind=kLoop, calls=%fused_computation | loop fusion | bytes 1179648 | tf_op jit(solution)/shard_map/transpose | solution.py:296
  (4 shorter events, 0.1 us)
Async XLA Ops:
  0.6 0.7 copy-start.1
  2.3 1.8 %copy-start = (bf16[48,24,128]{2,1,0:T(8,128)(2,1)S(1)}, bf16[48,24,128]{2,1,0:T(8,128)(2,1)}, u32[]{:S(2)}) copy-start(bf16[48,24,128]{2,1,0:T(8,128)(2,1)} %param.9) | copy-start | bytes 884740

commit v5 on v4

--- a/solution.py
+++ b/solution.py
@@ -46,7 +46,6 @@
         return carry
 
     lax.fori_loop(1, total, greet, 0)
-    pl.semaphore_wait(barrier, total - 1)
 
 
 def exchange(rows, cols, src, dst, send_sem, recv_sem, own_sem):
@@ -257,8 +256,9 @@
             rows, cols, src, dst, send_sem.at[phase], recv_sem.at[phase], own_sem.at[phase]
         )
 
+    greet_all(rows, cols)
     first(own, total, x, mask, w_in, proj, sides, 128)
-    greet_all(rows, cols)
+    pl.semaphore_wait(pltpu.get_barrier_semaphore(), total - 1)
     move(sides, sides_in, 0)
     forward_kernel(sizes, own, sides_in, outer_out, planes, plane, lines)
     move(outer_out, outer_in, 1)

time: 78.1 us -> 74.9 us (0.959)
  Pallas kernels: 70.7 us -> 67.9 us
    pallas_call x1, Pallas kernels: 70.7 us -> 67.9 us  [on_device(): pl.pallas_call(functools.partial(core_kernel, sizes, own), out_shape=(fla...]
where the time goes in v5:
time: 74.9 us; the launch traced here: 74.8 us
  Pallas kernels  67.9 us (91%)
  local copies, waits for them, and re-layouts  5.84 us (8%)
    pallas_call x1, Pallas kernels, on_device(): pl.pallas_call(functools.partial(core_kernel, sizes, own), out_shape=(fla...  67.9 us
    transpose x2, local copies, waits for them, and re-layouts, turned(): return values.transpose(1, 0, 2).reshape(entries, width)  2.51 us
    transpose x1, local copies, waits for them, and re-layouts, home(): return values.reshape(tile_j, tile_i, width).transpose(1, 0, 2)  2.01 us

profile of v5, /device:TPU:15, one launch (start us, length us, event | category | flops | bytes accessed | tf_op | source)
XLA Modules:
  0.0 74.8 jit_solution(13725291704753945083)
XLA Ops:
  0.6 0.0 copy-start.1
  0.7 0.6 copy-done.1
  1.3 0.1 select_reduce_fusion.1
  1.4 0.1 select_reduce_fusion
  1.5 0.1 broadcast_multiply_fusion
  1.6 0.7 mul.51.mask
  2.3 0.0 copy-start
  2.3 1.8 %copy.11 = bf16[24,48,128]{2,1,0:T(8,128)(2,1)} copy(bf16[24,48,128]{2,0,1:T(8,128)(2,1)} %bitcast.12) | data formatting | bytes 589824 | tf_op jit(solution)/shard_map/transpose | solution.py:293
  4.0 0.0 copy-done
  4.0 0.8 %copy.12 = bf16[24,48,128]{2,1,0:T(8,128)(2,1)} copy(bf16[24,48,128]{2,0,1:T(8,128)(2,1)S(1)} %bitcast.13) | data formatting | bytes 589824 | tf_op jit(solution)/shard_map/transpose | solution.py:293
  4.8 67.9 %core.1 = (bf16[1152,128]{1,0:T(8,128)(2,1)}, bf16[1152,128]{1,0:T(8,128)(2,1)}) custom-call(bf16[1152,128]{1,0:T(8,128)(2,1)} %bitcast.10, f32[1,1152]{1,0:T(1,128)} %mul.51.mask, bf16[128,640]{1,0:T(8,128)(2,1)} %w_in.1, bf16[128,128]{1,0:T(8,128)(2,1)} %w_out.1, bf16[1152,128]{1,0:T(8,128)(2,1)} %bitcast.11), custom_call_target="tpu_custom_call" | custom-call | tf_op jit(solution)/shard_map/core/pallas_call | solution.py:299
  72.7 2.0 %copy_bitcast_fusion = (bf16[48,24,128]{2,1,0:T(8,128)(2,1)}, bf16[48,24,128]{2,1,0:T(8,128)(2,1)}) fusion(bf16[24,48,128]{2,1,0:T(8,128)(2,1)} %bitcast.15, bf16[24,48,128]{2,1,0:T(8,128)(2,1)} %bitcast.14), kind=kLoop, calls=%fused_computation | loop fusion | bytes 1179648 | tf_op jit(solution)/shard_map/transpose | solution.py:296
  (4 shorter events, 0.1 us)
Async XLA Ops:
  0.6 0.7 copy-start.1
  2.3 1.8 %copy-start = (bf16[48,24,128]{2,1,0:T(8,128)(2,1)S(1)}, bf16[48,24,128]{2,1,0:T(8,128)(2,1)}, u32[]{:S(2)}) copy-start(bf16[48,24,128]{2,1,0:T(8,128)(2,1)} %param.9) | copy-start | bytes 884740
